TPU v7x, 256 devices: a whole 4x4x8 slice. The times are simulated.
256 devices in a mesh: dp: 64 (over x, y_hi, z), head: 2 (over core), side: 2 (over y_lo).
Axes of the slice: x: 4, y: 4 (y_hi: 2, y_lo: 2; y = y_hi * 2 + y_lo), z: 8, core: 2. Of those that a mesh axis runs over, the one named last changes fastest.
Arguments:
- queries: bfloat16 [2, 192, 8192], P('side', 'dp', 'head'), may hold values from -160 to 160
- new_keys: bfloat16 [2, 192, 512], P('side', 'dp', 'head'), may hold values from -6 to 6
- new_values: bfloat16 [2, 192, 512], P('side', 'dp', 'head'), may hold values from -6 to 6
- key_cache: bfloat16 [2, 192, 2048, 512], P('side', 'dp', None, 'head'), may hold values from -6 to 6
- value_cache: bfloat16 [2, 192, 2048, 512], P('side', 'dp', None, 'head'), may hold values from -6 to 6
- cache_lengths: int32 [2, 192], P('side', 'dp'), may hold values from 1 to 2048, 196608 in all within a row
- residual: bfloat16 [2, 192, 16384], P(None, None, 'dp'), may hold values from -32 to 32
- norm_gain: bfloat16 [16384], P('dp'), may hold values from 0.099609375 to 1.8984375
- out_weight: bfloat16 [8192, 16384], P(('head', 'side'), 'dp'), may hold values from -0.0625 to 0.0625
- gate_weight: bfloat16 [16384, 13312], P('dp', ('head', 'side')), may hold values from -0.046875 to 0.046875
- up_weight: bfloat16 [16384, 13312], P('dp', ('head', 'side')), may hold values from -0.046875 to 0.046875
- down_weight: bfloat16 [13312, 16384], P(('head', 'side'), 'dp'), may hold values from -0.0546875 to 0.0546875
Outputs:
- layer_out: bfloat16 [2, 192, 16384], P('side', 'dp')
Inputs may be any that keep to these rules, and one draw needn't show every extreme that they name: `cache_lengths`: A single row holds 1 to 2048 cached positions. Over the 192 rows of one micro-batch (one line of this array) the lengths add up to 196608, and the longest row of each micro-batch holds exactly 2048.
All inputs are finite; a program needn't handle non-finite values. No bound on the sum of `cache_lengths` on one device may be relied on, other than what follows from the above.
Results may differ from a plain program's by a relative error of at most 0.02.
Values may be sent and summed in bfloat16 or wider, within the bound.
A program may use at most 128 MiB of HBM per device.

v0:
```python
import math

import jax
import jax.numpy as jnp
from jax import lax
from jax.sharding import PartitionSpec as P

D = 16384
HS = 128
QH = 64
KVH = 4


def attend(queries, new_keys, new_values, key_cache, value_cache, cache_lengths):
    row_count = queries.shape[1]
    span = key_cache.shape[2]
    kv_local = key_cache.shape[3] // HS
    group = QH // KVH
    query_heads = queries[0].reshape(row_count, kv_local, group, HS)
    cache_keys = key_cache[0].reshape(row_count, span, kv_local, HS)
    cache_values = value_cache[0].reshape(row_count, span, kv_local, HS)
    fresh_key = new_keys[0].reshape(row_count, kv_local, HS)
    fresh_value = new_values[0].reshape(row_count, kv_local, HS).astype(jnp.float32)
    scale_factor = 1.0 / math.sqrt(HS)
    scores = (
        jnp.einsum("rjgd,rtjd->rjgt", query_heads, cache_keys, preferred_element_type=jnp.float32)
        * scale_factor
    )
    fresh = (
        jnp.einsum("rjgd,rjd->rjg", query_heads, fresh_key, preferred_element_type=jnp.float32)
        * scale_factor
    )
    valid = lax.broadcasted_iota(jnp.int32, (row_count, span), 1) < cache_lengths[0][:, None]
    masked = jnp.where(valid[:, None, None, :], scores, -jnp.inf)
    highest = jnp.maximum(jnp.max(masked, axis=-1), fresh)
    probs = jnp.exp(masked - highest[..., None])
    fresh_prob = jnp.exp(fresh - highest)
    total = jnp.sum(probs, axis=-1) + fresh_prob
    weights = (probs / total[..., None]).astype(jnp.bfloat16)
    fresh_weight = (fresh_prob / total).astype(jnp.bfloat16)
    mixed = jnp.einsum("rjgt,rtjd->rjgd", weights, cache_values, preferred_element_type=jnp.float32)
    mixed = mixed + fresh_weight.astype(jnp.float32)[..., None] * fresh_value[:, :, None, :]
    return mixed.reshape(1, row_count, kv_local * group * HS).astype(jnp.bfloat16)


def body(
    queries,
    new_keys,
    new_values,
    key_cache,
    value_cache,
    cache_lengths,
    residual,
    norm_gain,
    out_weight,
    gate_weight,
    up_weight,
    down_weight,
):
    attended = attend(queries, new_keys, new_values, key_cache, value_cache, cache_lengths)
    regrouped = lax.all_to_all(attended, "side", split_axis=2, concat_axis=0, tiled=True)
    projected = jnp.einsum(
        "ohs,sn->ohn",
        lax.all_gather(regrouped, "dp", axis=1, tiled=True),
        out_weight,
        preferred_element_type=jnp.float32,
    )
    projected = lax.psum(projected.astype(jnp.bfloat16), ("head", "side")).astype(jnp.float32)
    hidden_in = residual.astype(jnp.float32) + projected
    squares = lax.psum(jnp.sum(hidden_in * hidden_in, axis=-1), "dp")
    scaling = lax.rsqrt(squares / D + 1e-05)
    normed = (hidden_in * scaling[..., None] * norm_gain.astype(jnp.float32)).astype(jnp.bfloat16)
    batch_count = normed.shape[0]
    width_local = normed.shape[2]
    flat_rows = normed.reshape(batch_count * normed.shape[1], width_local)
    gate = jnp.dot(flat_rows, gate_weight, preferred_element_type=jnp.float32)
    upper = jnp.dot(flat_rows, up_weight, preferred_element_type=jnp.float32)
    mine = lax.psum_scatter(jnp.stack([gate, upper], axis=1), "dp", scatter_dimension=0, tiled=True)
    act_rows = (jax.nn.silu(mine[:, 0]) * mine[:, 1]).astype(jnp.bfloat16)
    lowered = jnp.dot(
        lax.all_gather(act_rows, "dp", axis=0, tiled=True),
        down_weight,
        preferred_element_type=jnp.float32,
    )
    lowered = lowered.reshape(batch_count, normed.shape[1], width_local)
    summed = lax.psum(lowered.astype(jnp.bfloat16), ("head", "side")).astype(jnp.float32)
    finished = (hidden_in + summed).astype(jnp.bfloat16)
    returned = lax.all_to_all(finished, "dp", split_axis=1, concat_axis=2, tiled=True)
    return lax.dynamic_slice_in_dim(returned, lax.axis_index("side"), 1, 0)


def solution(mesh):
    return jax.shard_map(
        body,
        mesh=mesh,
        in_specs=(
            P("side", "dp", "head"),
            P("side", "dp", "head"),
            P("side", "dp", "head"),
            P("side", "dp", None, "head"),
            P("side", "dp", None, "head"),
            P("side", "dp"),
            P(None, None, "dp"),
            P("dp"),
            P(("head", "side"), "dp"),
            P("dp", ("head", "side")),
            P("dp", ("head", "side")),
            P(("head", "side"), "dp"),
        ),
        out_specs=P("side", "dp", None),
        check_vma=False,
    )
```

profile of v0, /device:TPU:1, one launch (start us, length us, event | category | flops | bytes accessed | tf_op | source)
XLA Modules:
  0.0 1382.2 jit_solution(15612393245894653437)
XLA Ops:
  6.5 0.9 copy.50
  7.4 5.5 reshape_squeeze.14
  13.2 2.9 fusion.36
  16.4 5.5 reshape_squeeze.16
  22.0 2.5 fusion.19
  24.5 3.9 copy.36
  28.9 23.4 %reduce = bf16[4096,3]{1,0:T(8,128)(2,1)S(1)} reduce(bf16[4096,1,3]{2,1,0:T(2,128)(2,1)} %bitcast.75, bf16[]{:T(256)} %broadcast.14), dimensions={1}, to_apply=%bitcast.64.reduce_sub_computation | reduce | bytes 49154
  52.3 1.5 reshape.60
  53.8 5.9 all_to_all.36
  59.8 3.2 reshape.61
  63.0 4.6 copy.37
  68.3 116.3 %all-gather.5.cloned.1.call-done = bf16[2,1,192,2048]{3,0,1,2:T(2,128)(2,1)} async-done(((bf16[2,1,3,2048]{3,0,1,2:T(2,128)(2,1)}), bf16[2,1,192,2048]{3,0,1,2:T(2,128)(2,1)}) %all-gather.5.cloned.1.call-update) | async-done | bytes 1572880 | tf_op jit(solution)/shard_map/all_gather | solution.py:64
  184.6 3.4 fusion.13
  188.1 44.2 %all-reduce.5.cloned.1.call-done = bf16[2,192,256]{2,1,0:T(8,128)(2,1)} async-done(((bf16[2,192,256]{2,1,0:T(8,128)(2,1)}), bf16[2,192,256]{2,1,0:T(8,128)(2,1)}) %all-reduce.5.cloned.1.call-update) | async-done | bytes 196624 | tf_op jit(solution)/shard_map/psum | solution.py:68
  232.3 1.1 multiply_reduce_fusion
  233.4 156.3 %psum.22 = f32[2,192]{1,0:T(2,128)S(1)} all-reduce(f32[2,192]{1,0:T(2,128)S(1)} %multiply_reduce_fusion), channel_id=1, replica_groups=mesh['dp'=64,'head'=2,'side'=2] {'dp'}, use_global_device_ids=true, to_apply=%region_4.5 | all-reduce | flops 384 | bytes 3072 | tf_op jit(solution)/shard_map/psum | solution.py:70
  389.6 1.0 multiply_convert_fusion
  390.7 3.1 convolution_bitcast_fusion
  393.8 3.4 convolution_bitcast_fusion.1
  397.9 3.1 pad_maximum_fusion
  401.0 19.0 %copy.40 = f32[384,2,3328]{2,1,0:T(2,128)} copy(f32[384,2,3328]{2,0,1:T(8,128)S(1)} %pad_maximum_fusion) | data formatting | bytes 20447232 | tf_op jit(solution)/shard_map/stack | solution.py:78
  421.9 713.4 %all-reduce.9.cloned.1.call-done = f32[384,2,3328]{2,1,0:T(2,128)} async-done(((f32[384,2,3328]{2,1,0:T(2,128)}), f32[384,2,3328]{2,1,0:T(2,128)}) %all-reduce.9.cloned.1.call-update) | async-done | bytes 10223632
  1135.3 1.1 constant_dynamic-slice_fusion
  1137.2 157.7 %all-gather.7.cloned.1.call-done = bf16[64,6,3328]{2,1,0:T(8,128)(2,1)} async-done(((bf16[1,6,3328]{2,1,0:T(8,128)(2,1)}), bf16[64,6,3328]{2,1,0:T(8,128)(2,1)}) %all-gather.7.cloned.1.call-update) | async-done | bytes 2555920 | tf_op jit(solution)/shard_map/all_gather | solution.py:81
  1294.9 5.5 reshape.53
  1300.4 3.8 convolution_convert_fusion
  1304.2 43.8 %all-reduce.7.cloned.1.call-done = bf16[2,192,256]{2,1,0:T(8,128)(2,1)} async-done(((bf16[2,192,256]{2,1,0:T(8,128)(2,1)}), bf16[2,192,256]{2,1,0:T(8,128)(2,1)}) %all-reduce.7.cloned.1.call-update) | async-done | bytes 196624 | tf_op jit(solution)/shard_map/psum | solution.py:86
  1348.0 1.0 add_convert_fusion
  1349.0 0.9 copy.42
  1349.9 12.3 all-to-all-start.1
  1362.2 12.3 all-to-all-done.1
  1374.8 0.8 copy.44
  (48 shorter events, 5.0 us)
Async XLA Ops:
  6.5 384.1 %copy-start = (bf16[256,3328]{1,0:T(8,128)(2,1)S(1)}, bf16[256,3328]{1,0:T(8,128)(2,1)}, u32[]{:S(2)}) copy-start(bf16[256,3328]{1,0:T(8,128)(2,1)} %param.22) | copy-start | bytes 5111812
  6.5 178.1 %all-gather.5.cloned.1.call-start = ((), (), s32[]{:S(2)}) async-start(), calls=%async_computation.4 | async-start | bytes 1597440 | tf_op jit(solution)/shard_map/all_gather | solution.py:64
  7.4 5.6 copy-start.8
  7.4 5.6 copy-start.6
  16.4 5.5 copy-start.7
  63.0 125.1 %copy-start.9 = (bf16[256]{0:T(256)(128)(2,1)S(1)}, bf16[256]{0:T(256)(128)(2,1)}, u32[]{:S(2)}) copy-start(bf16[256]{0:T(256)(128)(2,1)} %param.19) | copy-start | bytes 1540
  63.0 169.3 %copy-start.3 = (bf16[2,192,256]{2,1,0:T(8,128)(2,1)S(1)}, bf16[2,192,256]{2,1,0:T(8,128)(2,1)}, u32[]{:S(2)}) copy-start(bf16[2,192,256]{2,1,0:T(8,128)(2,1)} %param.18) | copy-start | bytes 589828
  68.3 164.0 %all-reduce.5.cloned.1.call-start = ((), (), s32[]{:S(2)}) async-start(), calls=%async_computation.2 | async-start | bytes 393216 | tf_op jit(solution)/shard_map/psum | solution.py:68
  188.0 947.3 %all-reduce.9.cloned.1.call-start = ((), (), s32[]{:S(2)}) async-start(), calls=%async_computation.6 | async-start | bytes 20447232
  390.7 3.1 copy-start.5
  393.8 4.1 copy-start.2
  420.0 0.7 copy-start.10
  420.0 874.9 %all-gather.7.cloned.1.call-start = ((), (), s32[]{:S(2)}) async-start(), calls=%async_computation.5 | async-start | bytes 3461120 | tf_op jit(solution)/shard_map/all_gather | solution.py:81
  1137.1 210.8 %all-reduce.7.cloned.1.call-start = ((), (), s32[]{:S(2)}) async-start(), calls=%async_computation.3 | async-start | bytes 393216 | tf_op jit(solution)/shard_map/psum | solution.py:86
  1294.9 80.7 %copy-start.1 = (bf16[256,3328]{1,0:T(8,128)(2,1)S(1)}, bf16[256,3328]{1,0:T(8,128)(2,1)}, u32[]{:S(2)}) copy-start(bf16[256,3328]{1,0:T(8,128)(2,1)} %param.22) | copy-start | bytes 5111812
  1300.4 47.6 %copy-start.4 = (bf16[2,192,256]{2,1,0:T(8,128)(2,1)S(1)}, bf16[2,192,256]{2,1,0:T(8,128)(2,1)}, u32[]{:S(2)}) copy-start(bf16[2,192,256]{2,1,0:T(8,128)(2,1)} %all-reduce.5.cloned.1.call-done) | copy-start | bytes 589828
  1349.9 24.6 %all-to-all-start.1 = ((bf16[2,192,256]{2,0,1:T(2,128)(2,1)}), bf16[2,192,256]{2,0,1:T(2,128)(2,1)S(1)}, u32[]{:S(2)}, u32[]{:S(2)}) async-start(bf16[2,192,256]{2,0,1:T(2,128)(2,1)} %copy.42), calls=%async_computation.1 | async-start | bytes 393216 | tf_op jit(solution)/shard_map/all_to_all | solution.py:88
Sparse Core Ops, SparseCore 0:
  68.4 116.1 all-gather.4
  188.2 44.0 all-reduce.4
  420.2 715.1 all-reduce.8
  1139.2 155.6 all-gather.6
  1304.3 43.6 all-reduce.6
where the time goes:
time: 1380 us
  waiting for transfers between devices  1090 us (79%)
  blocking collectives  162 us (12%)
  local copies, waits for them, and re-layouts  55.9 us (4%)
  other arithmetic  30.7 us (2%)
  matrix products  19.1 us (1%)
  between operations  13.9 us (1%)
    unnamed x6, waiting for transfers between devices  713 us
    all_gather x1, waiting for transfers between devices, body(): lax.all_gather(act_rows, 'dp', axis=0, tiled=True)  158 us
    psum x1, blocking collectives, body(): squares = lax.psum(jnp.sum(hidden_in * hidden_in, axis=-1), 'dp')  156 us
    all_gather x1, waiting for transfers between devices, body(): lax.all_gather(regrouped, 'dp', axis=1, tiled=True)  116 us
    psum x1, waiting for transfers between devices, body(): lax.psum(projected.astype(jnp.bfloat16), ('head', 'side'))  44.2 us
    psum x1, waiting for transfers between devices, body(): lax.psum(lowered.astype(jnp.bfloat16), ('head', 'side')).astype(jnp.float32)  43.8 us
  transfers between devices with their start and end apart: 6, of which 6 were waited for; matrix products, arithmetic and copies ran while one was open for 0% of the time, Pallas kernels for 0%

commit v1 on v0

v1 whole, which is shorter than its diff:
```python
import math

import jax
import jax.numpy as jnp
from jax import lax
from jax.experimental import pallas as pl
from jax.experimental.pallas import tpu as pltpu
from jax.sharding import PartitionSpec as P

D = 16384
HS = 128
BF = jnp.bfloat16
F32 = jnp.float32
MESH = pl.DeviceIdType.MESH
VMEM_LIMIT = 56 * 2**20

NA = 7
NB = 6


def attend_kernel(len_ref, q_ref, nk_ref, nv_ref, k_ref, v_ref, o_ref):
    row = pl.program_id(0)
    length = len_ref[0, row]
    span = k_ref.shape[1]
    q = q_ref[0].astype(F32)
    zero = jnp.zeros_like(q[:16])
    wide = jnp.concatenate(
        [jnp.concatenate([q[:16], zero], axis=1), jnp.concatenate([zero, q[16:]], axis=1)], axis=0
    )
    scale = 1.0 / math.sqrt(HS)
    nt = (((1,), (1,)), ((), ()))
    scores = lax.dot_general(wide.astype(BF), k_ref[0], nt, preferred_element_type=F32) * scale
    fresh = jnp.sum(wide * nk_ref[0].astype(F32), axis=1, keepdims=True) * scale
    valid = lax.broadcasted_iota(jnp.int32, (32, span), 1) < length
    masked = jnp.where(valid, scores, -jnp.inf)
    highest = jnp.maximum(jnp.max(masked, axis=1, keepdims=True), fresh)
    probs = jnp.exp(masked - highest)
    fresh_prob = jnp.exp(fresh - highest)
    total = jnp.sum(probs, axis=1, keepdims=True) + fresh_prob
    inverse = 1.0 / total
    weights = (probs * inverse).astype(BF)
    fresh_weight = (fresh_prob * inverse).astype(BF).astype(F32)
    mixed = jnp.dot(weights, v_ref[0], preferred_element_type=F32)
    mixed = mixed + fresh_weight * nv_ref[0].astype(F32)
    o_ref[0, 0] = mixed[:16, :HS].astype(BF)
    o_ref[0, 1] = mixed[16:, HS:].astype(BF)


def attend(queries, new_keys, new_values, key_cache, value_cache, cache_lengths):
    rows, span = key_cache.shape[1], key_cache.shape[2]
    return pl.pallas_call(
        attend_kernel,
        grid=(rows,),
        in_specs=[
            pl.BlockSpec(memory_space=pltpu.SMEM),
            pl.BlockSpec((1, 32, HS), lambda r: (r, 0, 0)),
            pl.BlockSpec((1, 1, 2 * HS), lambda r: (r, 0, 0)),
            pl.BlockSpec((1, 1, 2 * HS), lambda r: (r, 0, 0)),
            pl.BlockSpec((1, span, 2 * HS), lambda r: (r, 0, 0)),
            pl.BlockSpec((1, span, 2 * HS), lambda r: (r, 0, 0)),
        ],
        out_specs=pl.BlockSpec((1, 2, 16, HS), lambda r: (r, 0, 0, 0)),
        out_shape=jax.ShapeDtypeStruct((rows, 2, 16, HS), BF),
        compiler_params=pltpu.CompilerParams(vmem_limit_bytes=VMEM_LIMIT),
        cost_estimate=pl.CostEstimate(flops=2 * 2 * rows * 32 * span * 256, bytes_accessed=rows * span * 1024, transcendentals=rows * 32 * span),
        name="attend",
    )(
        cache_lengths,
        queries.reshape(rows, 32, HS),
        new_keys.reshape(rows, 1, 2 * HS),
        new_values.reshape(rows, 1, 2 * HS),
        key_cache[0],
        value_cache[0],
    )


def slab_kernel(
    att, res, gain, wo_hbm, wg_hbm, wu_hbm, wd_hbm,
    out,
    wo, wg, wu, wd,
    seen, wide, part, part_bf, quarter_in, hidden, scaled,
    squares, squares_in, squares_all,
    pa, pa_in1, pa_in2, ya, ya_in, za, za_in,
    pb, pb_in, xb, xb_in,
    act_a, act_b, down, down_bf, down_in, fin, send1, mid,
    wsem, ss, rs,
):
    dp = lax.axis_index("dp")
    h = lax.axis_index("head")
    s = lax.axis_index("side")
    z = lax.rem(dp, 8)
    xy = dp // 8
    yh = lax.rem(xy, 2)
    x = xy // 2
    mine = 2 * s + h

    def dev(dx=0, dy=0, dz=0, dh=0, ds=0):
        nx = lax.rem(x + (dx + 4), 4)
        ny = lax.rem(yh + dy, 2)
        nz = lax.rem(z + (dz + 8), 8)
        return ((nx * 2 + ny) * 8 + nz, lax.rem(h + dh, 2), lax.rem(s + ds, 2))

    counter = [0]
    pending = []

    def ids(count):
        first = counter[0]
        counter[0] += count
        return first

    def send(src, dst, target, index, keep=True):
        copy = pltpu.make_async_remote_copy(
            src_ref=src, dst_ref=dst, send_sem=ss.at[index], recv_sem=rs.at[index],
            device_id=target, device_id_type=MESH,
        )
        copy.start()
        if keep:
            pending.append(copy)
        return copy

    def arrived(ref, index):
        pltpu.make_async_remote_copy(
            src_ref=ref, dst_ref=ref, send_sem=ss.at[index], recv_sem=rs.at[index],
            device_id=dev(dh=1), device_id_type=MESH,
        ).wait_recv()

    def left(ref, index):
        pltpu.make_async_remote_copy(
            src_ref=ref, dst_ref=ref, send_sem=ss.at[index], recv_sem=rs.at[index],
            device_id=dev(dh=1), device_id_type=MESH,
        ).wait_send()

    loads = []
    for k, (src, dst) in enumerate(((wo_hbm, wo), (wg_hbm, wg), (wu_hbm, wu), (wd_hbm, wd))):
        copy = pltpu.make_async_copy(src, dst, wsem.at[k])
        copy.start()
        loads.append(copy)

    plane = [(dx, dy) for dx in range(4) for dy in range(2)]
    peers = [dict(dx=dx, dy=dy, dh=dh) for dx, dy in plane for dh in range(2) if dx or dy or dh]
    peers += [dict(dz=dz) for dz in range(1, 8)]
    peers += [dict(ds=1), dict(dh=1, ds=1)]
    barrier = pltpu.get_barrier_semaphore()
    for peer in peers:
        pl.semaphore_signal(barrier, inc=1, device_id=dev(**peer), device_id_type=MESH)
    pl.semaphore_wait(barrier, len(peers))

    side_id = ids(1)
    send(att.at[:, 1 - s], seen.at[s, dp], dev(ds=1), side_id)
    seen[s, dp] = att[:, s]

    y_id = ids(1)
    za_id = ids(8)
    xa_id = ids(8 * 3)
    xyb_id = ids(8)
    zb_id = ids(16)

    def block_a():
        send(seen.at[0, dp], seen.at[0, dp], dev(dy=1), y_id)

    def block_b():
        for k, (dx, dy) in enumerate(plane[1:]):
            send(seen.at[1, dp], seen.at[1, dp], dev(dx=dx, dy=dy), xyb_id + k)

    def slot(nx, ny, nz):
        return (nx * 2 + ny) * 8 + nz

    xs = [lax.rem(x + d, 4) for d in range(4)]
    zs = [lax.rem(z + d, 8) for d in range(8)]
    ys = [yh, 1 - yh]

    arrived(seen.at[1 - s, dp], side_id)
    block_a()
    block_b()

    seen5 = seen
    arrived(seen5.at[0, slot(x, ys[1], z)], y_id)

    def pair_ref(nx, nz):
        return seen8.at[nx, :, nz]

    seen8 = seen.at[0].reshape(4, 2, 8, 3, 16, HS)
    for d in range(1, 8):
        send(pair_ref(x, z), pair_ref(x, z), dev(dz=d), za_id + d)
    for j in range(1, 4):
        send(pair_ref(x, z), pair_ref(x, z), dev(dx=j), xa_id + j - 1)

    for k, (dx, dy) in enumerate(plane[1:]):
        arrived(seen.at[1, slot(lax.rem(x + 4 - dx, 4), lax.rem(yh + dy, 2), z)], xyb_id + k)
    seenz = seen.at[1].reshape(8, 8, 3, 16, HS)

    def ring(step, towards):
        src = lax.rem(z + 8 - towards * (step - 1), 8)
        if step == 4:
            return seenz.at[pl.ds(0 if towards > 0 else 4, 4), src]
        return seenz.at[:, src]

    def ring_in(step, towards):
        src = lax.rem(z + 8 - towards * step, 8)
        if step == 4:
            return seenz.at[pl.ds(0 if towards > 0 else 4, 4), src]
        return seenz.at[:, src]

    def ring_id(step, towards):
        return zb_id + step * 2 + (0 if towards > 0 else 1)

    for t in (1, -1):
        send(ring(1, t), ring(1, t), dev(dz=t), ring_id(0, t))

    a_order = [1, 7, 2, 6, 3, 5, 4]
    plan = {1: a_order[:2], 2: a_order[2:4], 3: a_order[4:6], 4: a_order[6:]}
    for step in range(1, 5):
        for d in plan[step]:
            nz = lax.rem(z + 8 - d, 8)
            arrived(pair_ref(x, nz), za_id + d)
            for j in range(1, 4):
                send(pair_ref(x, nz), pair_ref(x, nz), dev(dx=j), xa_id + 3 * d + j - 1)
        for t in (1, -1):
            arrived(ring_in(step, t), ring_id(step - 1, t))
            if step < 4:
                send(ring(step + 1, t), ring(step + 1, t), dev(dz=t), ring_id(step, t))

    loads[0].wait()

    def project(m):
        wide[...] = seen[m].reshape(64 * 3 * 16, HS).astype(F32)
        total = jnp.zeros((192, 256), F32)
        for g in range(8):
            left_half = wide[pl.ds(2 * g, 192, stride=16), :]
            right_half = wide[pl.ds(2 * g + 1, 192, stride=16), :]
            piece = jnp.concatenate([left_half, right_half], axis=1).astype(BF)
            total = total + jnp.dot(piece, wo[256 * g : 256 * g + 256, :], preferred_element_type=F32)
        for k in range(2):
            part[2 * m + k] = total[96 * k : 96 * k + 96]
            part_bf[2 * m + k] = total[96 * k : 96 * k + 96].astype(BF)

    project(1)
    for d in range(8):
        nz = lax.rem(z + 8 - d, 8)
        for j in range(1, 4):
            arrived(pair_ref(lax.rem(x + 4 - j, 4), nz), xa_id + 3 * d + j - 1)
    project(0)

    group = [(1, 0), (0, 1), (1, 1)]
    q1 = ids(3)
    for k, (dh, ds) in enumerate(group):
        there = 2 * lax.rem(s + ds, 2) + lax.rem(h + dh, 2)
        send(part_bf.at[there], quarter_in.at[k], dev(dh=dh, ds=ds), q1 + k)
    total = res[mine].astype(F32) + part[mine]
    for k in range(3):
        arrived(quarter_in.at[k], q1 + k)
        total = total + quarter_in[k].astype(F32)
    hidden[...] = total
    scaled[mine] = (total * gain[...].astype(F32)).astype(BF)
    q2 = ids(3)
    for k, (dh, ds) in enumerate(group):
        send(scaled.at[mine], scaled.at[mine], dev(dh=dh, ds=ds), q2 + k)

    row_square = jnp.sum(total * total, axis=1, keepdims=True)
    diagonal = lax.broadcasted_iota(jnp.int32, (96, 128), 0) == lax.broadcasted_iota(jnp.int32, (96, 128), 1)
    lanes = jnp.sum(jnp.where(diagonal, row_square, 0.0), axis=0, keepdims=True)
    squares[0] = jnp.broadcast_to(lanes, (8, 128))
    sx, sy, sz, sq = ids(3), ids(1), ids(7), ids(3)
    for j in range(1, 4):
        send(squares.at[0], squares_in.at[j - 1], dev(dx=j), sx + j - 1)

    def squares_x():
        for j in range(3):
            arrived(squares_in.at[j], sx + j)
        squares[1] = squares[0] + squares_in[0] + squares_in[1] + squares_in[2]
        send(squares.at[1], squares_in.at[3], dev(dy=1), sy)

    def squares_y():
        arrived(squares_in.at[3], sy)
        squares[2] = squares[1] + squares_in[3]
        for d in range(1, 8):
            send(squares.at[2], squares_in.at[3 + d], dev(dz=d), sz + d - 1)

    def squares_z():
        value = squares[2]
        for d in range(1, 8):
            arrived(squares_in.at[3 + d], sz + d - 1)
            value = value + squares_in[3 + d]
        squares_all[mine] = value
        for k, (dh, ds) in enumerate(group):
            send(squares_all.at[mine], squares_all.at[mine], dev(dh=dh, ds=ds), sq + k)

    def squares_done():
        for k, (dh, ds) in enumerate(group):
            arrived(squares_all.at[2 * lax.rem(s + ds, 2) + lax.rem(h + dh, 2)], sq + k)

    for k, (dh, ds) in enumerate(group):
        arrived(scaled.at[2 * lax.rem(s + ds, 2) + lax.rem(h + dh, 2)], q2 + k)

    rows = scaled[...].reshape(384, 256)
    loads[1].wait()
    loads[2].wait()
    xa1, xa2, xa3 = ids(4), ids(4), ids(4)
    zb = ids(16)
    ya_id, zra = ids(2), ids(14)
    xyr = ids(14)
    weight = (wg, wu)
    back = [lax.rem(x + 4 - d, 4) for d in range(4)]

    def multiply_a(u):
        for p in range(NA):
            value = jnp.dot(rows, weight[u][:, 256 * p : 256 * p + 256], preferred_element_type=F32)
            pa[u, :, :, p] = value.astype(BF).reshape(4, 2, 48, 256)
        send(pa.at[u, xs[2], 0], pa_in1.at[u, 0], dev(dx=1), xa1 + 2 * u)
        send(pa.at[u, xs[2], 1], pa_in1.at[u, 1], dev(dx=-1), xa1 + 2 * u + 1)
        send(pa.at[u, xs[1], 1], pa_in2.at[u, 0, 1], dev(dx=1), xa2 + 2 * u)
        send(pa.at[u, xs[3], 0], pa_in2.at[u, 1, 0], dev(dx=-1), xa2 + 2 * u + 1)

    def z_block(u, dist, towards):
        there = lax.rem(z + 8 + towards * dist, 8)
        if dist == 4:
            return pb.at[u, there, pl.ds(0 if towards > 0 else 3, 3)]
        return pb.at[u, there]

    def z_in(u, dist, towards):
        dst = pb_in.at[u, 0 if towards > 0 else 1, dist - 1]
        if dist == 4:
            return dst.at[pl.ds(0 if towards > 0 else 3, 3)]
        return dst

    def z_id(u, dist, towards):
        return zb + 8 * u + 2 * (dist - 1) + (0 if towards > 0 else 1)

    def z_send(u, dist):
        for t in (1, -1):
            send(z_block(u, dist, t), z_in(u, dist, t), dev(dz=t), z_id(u, dist, t))

    def multiply_b(u):
        for p in range(NB):
            c = NA + p
            value = jnp.dot(rows, weight[u][:, 256 * c : 256 * c + 256], preferred_element_type=F32)
            pb[u, :, p] = value.astype(BF).reshape(8, 48, 256)
        z_send(u, 4)

    def z_step(u, dist):
        for t in (1, -1):
            arrived(z_in(u, dist, t), z_id(u, dist, t))
            there = lax.rem(z + 8 + t * (dist - 1), 8)
            d = 0 if t > 0 else 1
            if dist == 4:
                lo = 0 if t > 0 else 3
                pb[u, there, lo : lo + 3] = (
                    pb[u, there, lo : lo + 3].astype(F32) + pb_in[u, d, 3, lo : lo + 3].astype(F32)
                ).astype(BF)
            else:
                pb[u, there] = (pb[u, there].astype(F32) + pb_in[u, d, dist - 1].astype(F32)).astype(BF)
        z_send(u, dist - 1)

    def x_step(u):
        arrived(pa_in1.at[u, 0], xa1 + 2 * u)
        pa[u, xs[1], 0] = (pa[u, xs[1], 0].astype(F32) + pa_in1[u, 0].astype(F32)).astype(BF)
        send(pa.at[u, xs[1], 0], pa_in2.at[u, 0, 0], dev(dx=1), xa3 + 2 * u)
        arrived(pa_in1.at[u, 1], xa1 + 2 * u + 1)
        pa[u, xs[3], 1] = (pa[u, xs[3], 1].astype(F32) + pa_in1[u, 1].astype(F32)).astype(BF)
        send(pa.at[u, xs[3], 1], pa_in2.at[u, 1, 1], dev(dx=-1), xa3 + 2 * u + 1)

    def x_sum(u, ny):
        return pa[u, x, ny].astype(F32) + pa_in2[u, 0, ny].astype(F32) + pa_in2[u, 1, ny].astype(F32)

    def x_done(u):
        arrived(pa_in2.at[u, 0, 1], xa2 + 2 * u)
        arrived(pa_in2.at[u, 1, 0], xa2 + 2 * u + 1)
        arrived(pa_in2.at[u, 0, 0], xa3 + 2 * u)
        arrived(pa_in2.at[u, 1, 1], xa3 + 2 * u + 1)
        ya[u] = x_sum(u, ys[1]).astype(BF)
        send(ya.at[u], ya_in.at[u], dev(dy=1), ya_id + u)

    def y_done(u):
        arrived(ya_in.at[u], ya_id + u)
        za[u] = (x_sum(u, yh) + ya_in[u].astype(F32)).astype(BF)
        for d in range(1, 8):
            there = zs[d]

            @pl.when(there < NA)
            def _():
                send(za.at[u, there], za_in.at[u, d - 1], dev(dz=d), zra + 7 * u + d - 1, keep=False)

    def xb_start(u):
        for t in (1, -1):
            arrived(z_in(u, 1, t), z_id(u, 1, t))
        xb[u] = (
            pb[u, z].astype(F32) + pb_in[u, 0, 0].astype(F32) + pb_in[u, 1, 0].astype(F32)
        ).astype(BF)
        for k, (dx, dy) in enumerate(plane[1:]):
            there = 2 * xs[dx] + ys[dy]

            @pl.when(there < NB)
            def _():
                send(xb.at[u, there], xb_in.at[u, k], dev(dx=dx, dy=dy), xyr + 7 * u + k, keep=False)

    for u in range(2):
        multiply_a(u)
        multiply_b(u)
    squares_x()
    for u in range(2):
        z_step(u, 4)
        x_step(u)
    squares_y()
    z_step(0, 3)
    z_step(1, 3)
    squares_z()
    x_done(0)
    z_step(0, 2)
    y_done(0)
    z_step(1, 2)
    squares_done()
    x_done(1)
    xb_start(0)
    y_done(1)
    xb_start(1)

    def scaling(index, offset):
        lane_scale = lax.rsqrt(squares_all[index][:1] / D + 1e-05)
        pick = (
            lax.broadcasted_iota(jnp.int32, (48, 128), 0) + offset
            == lax.broadcasted_iota(jnp.int32, (48, 128), 1)
        )
        return jnp.sum(jnp.where(pick, lane_scale, 0.0), axis=1, keepdims=True)

    def activate(gate, upper, scale):
        gate = gate * scale
        return (gate / (1.0 + jnp.exp(-gate)) * (upper * scale)).astype(BF)

    ga, gay, gax = ids(8), ids(8), ids(42)
    gb, gbz = ids(8), ids(16)

    @pl.when(z < NA)
    def _():
        sums = []
        for u in range(2):
            value = za[u, lax.rem(z, NA)].astype(F32)
            for d in range(1, 8):
                arrived(za_in.at[u, d - 1], zra + 7 * u + d - 1)
                value = value + za_in[u, d - 1].astype(F32)
            sums.append(value)
        act_a[xy, z] = activate(sums[0], sums[1], scaling(x, 48 * yh))
        for d in range(1, 8):
            send(act_a.at[xy, z], act_a.at[xy, z], dev(dz=d), ga + d, keep=False)

    @pl.when(xy < NB)
    def _():
        sums = []
        for u in range(2):
            value = xb[u, xy].astype(F32)
            for k in range(7):
                arrived(xb_in.at[u, k], xyr + 7 * u + k)
                value = value + xb_in[u, k].astype(F32)
            sums.append(value)
        act_b[z, xy] = activate(sums[0], sums[1], scaling(z // 2, 48 * lax.rem(z, 2)))
        for k, (dx, dy) in enumerate(plane[1:]):
            send(act_b.at[z, xy], act_b.at[z, xy], dev(dx=dx, dy=dy), gb + k, keep=False)

    for k, (dx, dy) in enumerate(plane[1:]):
        there = 2 * back[dx] + ys[dy]

        @pl.when(there < NB)
        def _():
            arrived(act_b.at[z, there], gb + k)

    def gz(step, towards, shift):
        src = lax.rem(z + 8 - towards * (step - 1 + shift), 8)
        if step == 4:
            return act_b.at[src, pl.ds(0 if towards > 0 else 3, 3)]
        return act_b.at[src]

    def gz_id(step, towards):
        return gbz + 2 * step + (0 if towards > 0 else 1)

    for t in (1, -1):
        send(gz(1, t, 0), gz(1, t, 0), dev(dz=t), gz_id(0, t))

    order = [0, 1, 7, 2, 6, 3, 5, 4]

    def a_ref(nx, ny, nz):
        return act_a.at[2 * nx + ny, nz]

    def a_step(d):
        nz = lax.rem(z + 8 - d, 8)

        @pl.when(nz < NA)
        def _():
            if d > 0:
                arrived(a_ref(x, yh, nz), ga + d)
            send(a_ref(x, yh, nz), a_ref(x, yh, nz), dev(dy=1), gay + d, keep=False)

    def pair_a(nx, nz):
        return act_a.at[pl.ds(2 * nx, 2), nz]

    def a_step2(d):
        nz = lax.rem(z + 8 - d, 8)

        @pl.when(nz < NA)
        def _():
            arrived(a_ref(x, ys[1], nz), gay + d)
            for j in range(1, 4):
                send(pair_a(x, nz), pair_a(x, nz), dev(dx=j), gax + 3 * d + j - 1 if d < 8 else 0, keep=False)

    a_step(0)
    a_step(1)
    a_step(7)
    a_step2(0)
    a_step(2)
    a_step(6)
    a_step2(1)
    a_step2(7)
    for step in range(1, 5):
        for t in (1, -1):
            arrived(gz(step, t, 1), gz_id(step - 1, t))
            if step < 4:
                send(gz(step + 1, t, 0), gz(step + 1, t, 0), dev(dz=t), gz_id(step, t))
        if step == 1:
            a_step(3)
            a_step(5)
            a_step(4)
            a_step2(2)
            a_step2(6)
        if step == 2:
            a_step2(3)
            a_step2(5)
            a_step2(4)

    loads[3].wait()
    value = jnp.zeros((384, 256), F32)
    for p in range(NB):
        block = act_b[:, p].reshape(384, 256)
        value = value + jnp.dot(block, wd[256 * (NA + p) : 256 * (NA + p) + 256, :], preferred_element_type=F32)
    down[...] = value.reshape(4, 96, 256)
    for d in range(8):
        nz = lax.rem(z + 8 - d, 8)

        @pl.when(nz < NA)
        def _():
            for j in range(1, 4):
                arrived(pair_a(back[j], nz), gax + 3 * d + j - 1)

    value = down[...].reshape(384, 256)
    for p in range(NA):
        block = act_a[:, p].reshape(384, 256)
        value = value + jnp.dot(block, wd[256 * p : 256 * p + 256, :], preferred_element_type=F32)
    down[...] = value.reshape(4, 96, 256)
    down_bf[...] = value.astype(BF).reshape(4, 96, 256)

    q3 = ids(3)
    for k, (dh, ds) in enumerate(group):
        there = 2 * lax.rem(s + ds, 2) + lax.rem(h + dh, 2)
        send(down_bf.at[there], down_in.at[k], dev(dh=dh, ds=ds), q3 + k)
    total = hidden[...] + down[mine]
    for k in range(3):
        arrived(down_in.at[k], q3 + k)
        total = total + down_in[k].astype(F32)
    fin[0] = total[:, :128]
    fin[1] = total[:, 128:]

    for r in range(3):
        for j in range(2):
            send1[pl.ds(2 * r + j, 32, stride=8), :] = fin[j, pl.ds(r, 32, stride=3), :]
    for j in range(2):
        send1[pl.ds(6 + j, 32, stride=8), :] = jnp.zeros((32, 128), F32)
    blocks = send1.reshape(4, 8, 8, 128)
    f1 = ids(7)
    for d in range(1, 8):
        send(blocks.at[:, zs[d]], mid.at[z], dev(dz=d), f1 + d - 1)
    mid[z] = blocks[:, z]
    for d in range(1, 8):
        arrived(mid.at[lax.rem(z + 8 - d, 8)], f1 + d - 1)

    f2 = ids(16)
    targets = []
    for xl in range(2):
        for ny in range(2):
            for nh in range(2):
                nx = 2 * h + xl
                own = (nx == x) & (ny == yh) & (nh == h)
                index = 4 * xl + 2 * ny + nh
                targets.append((2 * xl + ny, own, index))

                @pl.when(own)
                def _():
                    out[xy] = mid[:, 2 * xl + ny]

                @pl.when(jnp.logical_not(own))
                def _():
                    copy = pltpu.make_async_remote_copy(
                        src_ref=mid.at[:, 2 * xl + ny], dst_ref=out.at[xy], send_sem=ss.at[f2 + index],
                        recv_sem=rs.at[f2 + xy], device_id=((nx * 2 + ny) * 8 + z, nh, s), device_id_type=MESH,
                    )
                    copy.start()
    for k in range(8):
        own = (xy == k) & (h == x // 2)

        @pl.when(jnp.logical_not(own))
        def _():
            arrived(out.at[k], f2 + k)

    for block, own, index in targets:
        @pl.when(jnp.logical_not(own))
        def _():
            left(mid.at[:, block], f2 + index)
    for copy in pending:
        copy.wait_send()
    for d in range(1, 8):
        @pl.when(zs[d] < NA)
        def _():
            for u in range(2):
                left(za.at[u, 0], zra + 7 * u + d - 1)
    for k, (dx, dy) in enumerate(plane[1:]):
        @pl.when(2 * xs[dx] + ys[dy] < NB)
        def _():
            for u in range(2):
                left(xb.at[u, 0], xyr + 7 * u + k)

    @pl.when(z < NA)
    def _():
        for d in range(1, 8):
            left(act_a.at[0, 0], ga + d)

    @pl.when(xy < NB)
    def _():
        for k in range(7):
            left(act_b.at[0, 0], gb + k)

    for d in range(8):
        @pl.when(lax.rem(z + 8 - d, 8) < NA)
        def _():
            left(act_a.at[0, 0], gay + d)
            for j in range(1, 4):
                left(act_a.at[pl.ds(0, 2), 0], gax + 3 * d + j - 1)
    assert counter[0] <= SEMS


SEMS = 320


def slab(att, residual, gain, out_weight, gate_weight, up_weight, down_weight):
    vmem = pl.BlockSpec(memory_space=pltpu.VMEM)
    anywhere = pl.BlockSpec(memory_space=pl.ANY)
    scratch = [
        pltpu.VMEM((2048, 256), BF),
        pltpu.VMEM((256, 3328), BF),
        pltpu.VMEM((256, 3328), BF),
        pltpu.VMEM((3328, 256), BF),
        pltpu.VMEM((2, 64, 3, 16, HS), BF),
        pltpu.VMEM((64 * 3 * 16, HS), F32),
        pltpu.VMEM((4, 96, 256), F32),
        pltpu.VMEM((4, 96, 256), BF),
        pltpu.VMEM((3, 96, 256), BF),
        pltpu.VMEM((96, 256), F32),
        pltpu.VMEM((4, 96, 256), BF),
        pltpu.VMEM((3, 8, 128), F32),
        pltpu.VMEM((11, 8, 128), F32),
        pltpu.VMEM((4, 8, 128), F32),
        pltpu.VMEM((2, 4, 2, NA, 48, 256), BF),
        pltpu.VMEM((2, 2, NA, 48, 256), BF),
        pltpu.VMEM((2, 2, 2, NA, 48, 256), BF),
        pltpu.VMEM((2, NA, 48, 256), BF),
        pltpu.VMEM((2, NA, 48, 256), BF),
        pltpu.VMEM((2, NA, 48, 256), BF),
        pltpu.VMEM((2, 7, 48, 256), BF),
        pltpu.VMEM((2, 8, NB, 48, 256), BF),
        pltpu.VMEM((2, 2, 4, NB, 48, 256), BF),
        pltpu.VMEM((2, NB, 48, 256), BF),
        pltpu.VMEM((2, 7, 48, 256), BF),
        pltpu.VMEM((8, NA, 48, 256), BF),
        pltpu.VMEM((8, NB, 48, 256), BF),
        pltpu.VMEM((4, 96, 256), F32),
        pltpu.VMEM((4, 96, 256), BF),
        pltpu.VMEM((3, 96, 256), BF),
        pltpu.VMEM((2, 96, 128), F32),
        pltpu.VMEM((256, 128), F32),
        pltpu.VMEM((8, 4, 8, 128), F32),
        pltpu.SemaphoreType.DMA((4,)),
        pltpu.SemaphoreType.DMA((SEMS,)),
        pltpu.SemaphoreType.DMA((SEMS,)),
    ]
    return pl.pallas_call(
        slab_kernel,
        out_shape=jax.ShapeDtypeStruct((8, 8, 8, 128), F32),
        in_specs=[vmem, vmem, vmem, anywhere, anywhere, anywhere, anywhere],
        out_specs=vmem,
        scratch_shapes=scratch,
        compiler_params=pltpu.CompilerParams(collective_id=0, has_side_effects=True, vmem_limit_bytes=VMEM_LIMIT),
        cost_estimate=pl.CostEstimate(flops=2 * 384 * 256 * 12032, bytes_accessed=8 * 2**20, transcendentals=0),
        name="slab",
    )(att, residual.reshape(4, 96, 256), gain.reshape(1, 256), out_weight, gate_weight, up_weight, down_weight)


def body(
    queries,
    new_keys,
    new_values,
    key_cache,
    value_cache,
    cache_lengths,
    residual,
    norm_gain,
    out_weight,
    gate_weight,
    up_weight,
    down_weight,
):
    attended = attend(queries, new_keys, new_values, key_cache, value_cache, cache_lengths)
    rows = slab(attended, residual, norm_gain, out_weight, gate_weight, up_weight, down_weight)
    rows = rows.reshape(64, 8, HS)[:, :6].reshape(64, 3, 2 * HS)
    return rows.transpose(1, 0, 2).reshape(1, 3, D).astype(BF)


def solution(mesh):
    return jax.shard_map(
        body,
        mesh=mesh,
        in_specs=(
            P("side", "dp", "head"),
            P("side", "dp", "head"),
            P("side", "dp", "head"),
            P("side", "dp", None, "head"),
            P("side", "dp", None, "head"),
            P("side", "dp"),
            P(None, None, "dp"),
            P("dp"),
            P(("head", "side"), "dp"),
            P("dp", ("head", "side")),
            P("dp", ("head", "side")),
            P(("head", "side"), "dp"),
        ),
        out_specs=P("side", "dp", None),
        check_vma=False,
    )
```

time: 1380 us -> 152 us (0.11)
  waiting for transfers between devices: 1090 us -> 0 us
  blocking collectives: 162 us -> 0 us
  Pallas kernels: 0 us -> 145 us
  local copies, waits for them, and re-layouts: 55.9 us -> 5.9 us
  other arithmetic: 30.7 us -> 0.97 us
  matrix products: 19.1 us -> 0 us
  between operations: 13.9 us -> 0.02 us
    unnamed x6 -> x0, waiting for transfers between devices: 713 us -> none
    all_gather x2 -> x0, waiting for transfers between devices: 274 us -> none  [the longest x1 158 us: body(): lax.all_gather(act_rows, 'dp', axis=0, tiled=True)]
    psum x1 -> x0, blocking collectives: 156 us -> none  [body(): squares = lax.psum(jnp.sum(hidden_in * hidden_in, axis=-1), 'dp')]
    pallas_call x0 -> x2, Pallas kernels: none -> 145 us  [the longest x1 139 us: slab(): pl.pallas_call(slab_kernel, out_shape=jax.ShapeDtypeStruct((8, 8, 8, 128)...]
    psum x2 -> x0, waiting for transfers between devices: 88 us -> none  [the longest x1 44.2 us: body(): lax.psum(projected.astype(jnp.bfloat16), ('head', 'side'))]
    another operation x4 -> x0, local copies, waits for them, and re-layouts: 30.1 us -> none  [the longest x1 19 us: body(): jnp.stack([gate, upper], axis=1)]
    unnamed x2 -> x0, other arithmetic: 24.1 us -> none
    dot_general x7 -> x0, matrix products: 19.1 us -> none  [the longest x1 3.77 us: body(): jnp.dot(lax.all_gather(act_rows, 'dp', axis=0, tiled=True), down_weight,...]
  transfers between devices with their start and end apart: 6 -> 0, of which waited for: 6 -> 0; matrix products, arithmetic and copies ran while one was open for 0% -> 0% of each run, Pallas kernels for 0% -> 0%
where the time goes in v1:
time: 152 us
  Pallas kernels  145 us (95%)
  local copies, waits for them, and re-layouts  5.9 us (4%)
    pallas_call x1, Pallas kernels, slab(): pl.pallas_call(slab_kernel, out_shape=jax.ShapeDtypeStruct((8, 8, 8, 128)...  139 us
    pallas_call x1, Pallas kernels, attend(): pl.pallas_call(attend_kernel, grid=(rows,), in_specs=[pl.BlockSpec(memory...  5.92 us

profile of v1, /device:TPU:1, one launch (start us, length us, event | category | flops | bytes accessed | tf_op | source)
XLA Modules:
  0.0 151.7 jit_solution(18193110939843546825)
XLA Ops:
  0.0 1.2 reshape.39.gain
  1.2 1.3 copy.14.nk_ref
  2.5 1.3 copy.15.nv_ref
  3.8 1.4 copy.18
  5.2 5.9 %attend.1.att = bf16[3,2,16,128]{3,2,1,0:T(8,128)(2,1)} custom-call(s32[1,3]{1,0:T(1,128)} %len_ref.1, bf16[3,32,128]{2,1,0:T(8,128)(2,1)} %bitcast.18, bf16[3,1,256]{2,1,0:T(2,128)(2,1)} %copy.14.nk_ref, bf16[3,1,256]{2,1,0:T(2,128)(2,1)} %copy.15.nv_ref, bf16[3,2048,256]{2,1,0:T(8,128)(2,1)} %bitcast.15, bf16[3,2048,256]{2,1,0:T(8,128)(2,1)} %bitcast.16), custom_call_target="tpu_custom_call" | custom-call | flops 201326592 | bytes 6291456 | tf_op jit(solution)/shard_map/attend/pallas_call | solution.py:51
  11.1 138.8 %slab.1 = f32[8,8,8,128]{3,2,1,0:T(8,128)} custom-call(bf16[3,2,16,128]{3,2,1,0:T(8,128)(2,1)} %attend.1.att, bf16[4,96,256]{2,1,0:T(8,128)(2,1)} %bitcast.22, bf16[1,256]{1,0:T(2,128)(2,1)} %reshape.39.gain, bf16[2048,256]{1,0:T(8,128)(2,1)} %wo_hbm.1, bf16[256,3328]{1,0:T(8,128)(2,1)} %wg_hbm.1, bf16[256,3328]{1,0:T(8,128)(2,1)} %wu_hbm.1, ...), custom_call_target="tpu_custom_call" | custom-call | flops 2365587456 | bytes 8388608 | tf_op jit(solution)/shard_map/slab/pallas_call | solution.py:680
  149.9 1.0 convert.4
  150.9 0.8 convert_element_type.18

commit v2 on v1

v2 whole, which is shorter than its diff:
```python
import math

import jax
import jax.numpy as jnp
from jax import lax
from jax.experimental import pallas as pl
from jax.experimental.pallas import tpu as pltpu
from jax.sharding import PartitionSpec as P

D = 16384
HS = 128
BF = jnp.bfloat16
F32 = jnp.float32
MESH = pl.DeviceIdType.MESH
VMEM_LIMIT = 56 * 2**20

UNITS = 1664
NA = 8
NB = 5
PUSH = (1, 5, 2)
FLAT = 256


def attend_row(length, q, new_key, new_value, keys, values):
    span = keys.shape[0]
    zero = jnp.zeros((16, HS), F32)
    wide = jnp.concatenate(
        [jnp.concatenate([q[:16], zero], axis=1), jnp.concatenate([zero, q[16:]], axis=1)], axis=0
    )
    scale = 1.0 / math.sqrt(HS)
    nt = (((1,), (1,)), ((), ()))
    scores = lax.dot_general(wide.astype(BF), keys, nt, preferred_element_type=F32) * scale
    fresh = jnp.sum(wide * new_key, axis=1, keepdims=True) * scale
    valid = lax.broadcasted_iota(jnp.int32, (32, span), 1) < length
    masked = jnp.where(valid, scores, -jnp.inf)
    highest = jnp.maximum(jnp.max(masked, axis=1, keepdims=True), fresh)
    probs = jnp.exp(masked - highest)
    fresh_prob = jnp.exp(fresh - highest)
    total = jnp.sum(probs, axis=1, keepdims=True) + fresh_prob
    inverse = 1.0 / total
    weights = (probs * inverse).astype(BF)
    fresh_weight = (fresh_prob * inverse).astype(BF).astype(F32)
    mixed = jnp.dot(weights, values, preferred_element_type=F32) + fresh_weight * new_value
    return mixed[:16, :HS].astype(BF), mixed[16:, HS:].astype(BF)


def layer_kernel(
    lengths, queries, new_keys, new_values, key_hbm, value_hbm,
    res, gain, wo_hbm, wg_hbm, wu_hbm, wd_hbm,
    out,
    keys, values, att, wo, wg, wu, wd,
    seen, wide, part, part_bf, quarter_in, hidden, scaled,
    squares_mine, squares, squares_in, squares_all,
    pa, pa_in1, pa_in2, za, za_in,
    pb, pb_in, xb, xb_in, scale_rows,
    act_a, act_b, down, down_bf, down_in, fin, send1, mid,
    csem, wsem, ss, rs,
):
    dp = lax.axis_index("dp")
    h = lax.axis_index("head")
    s = lax.axis_index("side")
    z = lax.rem(dp, 8)
    xy = dp // 8
    yh = lax.rem(xy, 2)
    x = xy // 2
    mine = 2 * s + h

    def dev(dx=0, dy=0, dz=0, dh=0, ds=0):
        nx = lax.rem(x + (dx + 4), 4)
        ny = lax.rem(yh + dy, 2)
        nz = lax.rem(z + (dz + 8), 8)
        return ((nx * 2 + ny) * 8 + nz, lax.rem(h + dh, 2), lax.rem(s + ds, 2))

    counter = [0]
    pending = []

    def ids(count):
        first = counter[0]
        counter[0] += count
        return first

    def when(condition, action):
        if condition is None:
            action()
        else:
            pl.when(condition)(action)

    def copy_of(src, dst, target, send_index, recv_index):
        return pltpu.make_async_remote_copy(
            src_ref=src, dst_ref=dst, send_sem=ss.at[send_index], recv_sem=rs.at[recv_index],
            device_id=target, device_id_type=MESH,
        )

    def send(src, dst, target, index, condition=None, slot=None):
        when(condition, copy_of(src, dst, target, index, index if slot is None else slot).start)
        pending.append((src, index, condition))

    def arrived(ref, index):
        copy_of(ref, ref, dev(dh=1), index, index).wait_recv()

    caches = []
    for r in range(3):
        for k, (src, dst) in enumerate(((key_hbm, keys), (value_hbm, values))):
            copy = pltpu.make_async_copy(src.at[r], dst.at[r], csem.at[2 * r + k])
            copy.start()
            caches.append(copy)

    plane = [(dx, dy) for dx in range(4) for dy in range(2)]
    peers = [dict(dx=dx, dy=dy, dh=dh) for dx, dy in plane for dh in range(2) if dx or dy or dh]
    peers += [dict(dz=dz) for dz in range(1, 8)]
    peers += [dict(dy=dy, dh=dh, ds=1) for dy in range(2) for dh in range(2)]
    barrier = pltpu.get_barrier_semaphore()
    for peer in peers:
        pl.semaphore_signal(barrier, inc=1, device_id=dev(**peer), device_id_type=MESH)

    loads = []

    def load(src, dst):
        copy = pltpu.make_async_copy(src, dst, wsem.at[len(loads)])
        copy.start()
        loads.append(copy)

    units = pl.ds(pl.multiple_of(UNITS * yh, 128), UNITS)
    others = pl.ds(pl.multiple_of(UNITS * (1 - yh), 128), UNITS)
    w_id = ids(9)
    pieces = [
        (src.at[pl.ds(64 * k, 64), others], dst.at[yh, pl.ds(64 * k, 64)])
        for src, dst in ((wg_hbm, wg), (wu_hbm, wu)) for k in range(4)
    ]
    pushed = [0]

    def push(count):
        for _ in range(count):
            src, dst = pieces[pushed[0]]
            send(src, dst, dev(dy=1), w_id + pushed[0])
            pushed[0] += 1

    for r in range(3):
        q = queries[...].astype(F32)[r : r + 1]
        q = jnp.concatenate([q[:, HS * g : HS * g + HS] for g in range(32)], axis=0)
        caches[2 * r].wait()
        caches[2 * r + 1].wait()
        if r == 2:
            load(wo_hbm, wo)
            load(wg_hbm.at[:, units], wg.at[yh])
            load(wu_hbm.at[:, units], wu.at[yh])
            load(wd_hbm.at[units], wd.at[yh])
        low, high = attend_row(
            lengths[0, r], q, new_keys[...].astype(F32)[r : r + 1], new_values[...].astype(F32)[r : r + 1],
            keys[r], values[r],
        )
        att[r, 0] = low
        att[r, 1] = high
        if r == 0:
            pl.semaphore_wait(barrier, len(peers))
            push(PUSH[0])

    y_id = ids(4)
    for ny in range(2):
        for ns in range(2):
            if ny or ns:
                head = s if ns == 0 else 1 - s
                send(att.at[:, head], seen.at[s, dp], dev(dy=ny, ds=ns), y_id + 2 * ny + ns)
    seen[s, dp] = att[:, s]

    za_id = ids(8)
    xa_id = ids(8 * 3)
    xyb_id = ids(8)
    zb_id = ids(16)

    def slot(nx, ny, nz):
        return (nx * 2 + ny) * 8 + nz

    xs = [lax.rem(x + d, 4) for d in range(4)]
    zs = [lax.rem(z + d, 8) for d in range(8)]
    ys = [yh, 1 - yh]

    arrived(seen.at[1 - s, dp], y_id + 1)
    there = slot(x, ys[1], z)
    arrived(seen.at[s, there], y_id + 2)
    arrived(seen.at[1 - s, there], y_id + 3)

    push(PUSH[1])

    seen8 = seen.at[0].reshape(4, 2, 8, 3, 16, HS)

    def pair_ref(nx, nz):
        return seen8.at[nx, :, nz]

    for d in range(1, 8):
        send(pair_ref(x, z), pair_ref(x, z), dev(dz=d), za_id + d)
    for j in range(1, 4):
        send(pair_ref(x, z), pair_ref(x, z), dev(dx=j), xa_id + j - 1)

    seenx = seen.at[1].reshape(4, 2, 8, 3, 16, HS)
    for j in range(1, 4):
        send(seenx.at[x, :, z], seenx.at[x, :, z], dev(dx=j), xyb_id + j)
    for j in range(1, 4):
        arrived(seenx.at[lax.rem(x + 4 - j, 4), :, z], xyb_id + j)
    seenz = seen.at[1].reshape(8, 8, 3, 16, HS)

    def ring(step, towards):
        src = lax.rem(z + 8 - towards * (step - 1), 8)
        if step == 4:
            return seenz.at[pl.ds(0 if towards > 0 else 4, 4), src]
        return seenz.at[:, src]

    def ring_in(step, towards):
        src = lax.rem(z + 8 - towards * step, 8)
        if step == 4:
            return seenz.at[pl.ds(0 if towards > 0 else 4, 4), src]
        return seenz.at[:, src]

    def ring_id(step, towards):
        return zb_id + step * 2 + (0 if towards > 0 else 1)

    for t in (1, -1):
        send(ring(1, t), ring(1, t), dev(dz=t), ring_id(0, t))

    a_order = [1, 7, 2, 6, 3, 5, 4]
    plan = {1: a_order[:2], 2: a_order[2:4], 3: a_order[4:6], 4: a_order[6:]}
    for step in range(1, 5):
        for d in plan[step]:
            nz = lax.rem(z + 8 - d, 8)
            arrived(pair_ref(x, nz), za_id + d)
            for j in range(1, 4):
                send(pair_ref(x, nz), pair_ref(x, nz), dev(dx=j), xa_id + 3 * d + j - 1)
        for t in (1, -1):
            arrived(ring_in(step, t), ring_id(step - 1, t))
            if step < 4:
                send(ring(step + 1, t), ring(step + 1, t), dev(dz=t), ring_id(step, t))

    loads[0].wait()

    def project(m):
        wide[...] = seen[m].reshape(64 * 3 * 16, HS).astype(F32)
        total = jnp.zeros((192, 256), F32)
        for g in range(8):
            left_half = wide[pl.ds(2 * g, 192, stride=16), :]
            right_half = wide[pl.ds(2 * g + 1, 192, stride=16), :]
            piece = jnp.concatenate([left_half, right_half], axis=1).astype(BF)
            total = total + jnp.dot(piece, wo[256 * g : 256 * g + 256, :], preferred_element_type=F32)
        for k in range(2):
            part[2 * m + k] = total[96 * k : 96 * k + 96]
            part_bf[2 * m + k] = total[96 * k : 96 * k + 96].astype(BF)

    project(1)
    for d in range(8):
        nz = lax.rem(z + 8 - d, 8)
        for j in range(1, 4):
            arrived(pair_ref(lax.rem(x + 4 - j, 4), nz), xa_id + 3 * d + j - 1)
    project(0)

    group = [(1, 0), (0, 1), (1, 1)]
    q1 = ids(3)
    for k, (dh, ds) in enumerate(group):
        there = 2 * lax.rem(s + ds, 2) + lax.rem(h + dh, 2)
        send(part_bf.at[there], quarter_in.at[k], dev(dh=dh, ds=ds), q1 + k)
    total = res[mine].astype(F32) + part[mine]
    for k in range(3):
        arrived(quarter_in.at[k], q1 + k)
        total = total + quarter_in[k].astype(F32)
    hidden[...] = total
    scaled[yh, mine] = (total * gain[...].reshape(1, 256).astype(F32)).astype(BF)
    group8 = [(dy, dh, ds) for dy in range(2) for dh in range(2) for ds in range(2)][1:]
    q2 = ids(7)

    def quarter(dh, ds):
        return 2 * lax.rem(s + ds, 2) + lax.rem(h + dh, 2)

    for k, (dy, dh, ds) in enumerate(group8):
        send(scaled.at[yh, mine], scaled.at[yh, mine], dev(dy=dy, dh=dh, ds=ds), q2 + k)

    row_square = jnp.sum(total * total, axis=1, keepdims=True)
    diagonal = lax.broadcasted_iota(jnp.int32, (96, 128), 0) == lax.broadcasted_iota(jnp.int32, (96, 128), 1)
    lanes = jnp.sum(jnp.where(diagonal, row_square, 0.0), axis=0, keepdims=True)
    squares_mine[yh, mine] = jnp.broadcast_to(lanes, (8, 128))
    sg, sx, sz = ids(7), ids(3), ids(7)
    for k, (dy, dh, ds) in enumerate(group8):
        send(squares_mine.at[yh, mine], squares_mine.at[yh, mine], dev(dy=dy, dh=dh, ds=ds), sg + k)

    def squares_x():
        for k, (dy, dh, ds) in enumerate(group8):
            arrived(squares_mine.at[ys[dy], quarter(dh, ds)], sg + k)
        row = lax.broadcasted_iota(jnp.int32, (8, 128), 0)
        value = jnp.zeros((8, 128), F32)
        for k in range(4):
            value = value + jnp.where(row == k, squares_mine[0, k] + squares_mine[1, k], 0.0)
        squares[0] = value
        for j in range(1, 4):
            send(squares.at[0], squares_in.at[j - 1], dev(dx=j), sx + j - 1)

    def squares_z():
        for j in range(3):
            arrived(squares_in.at[j], sx + j)
        squares[1] = squares[0] + squares_in[0] + squares_in[1] + squares_in[2]
        for d in range(1, 8):
            send(squares.at[1], squares_in.at[2 + d], dev(dz=d), sz + d - 1)

    def squares_done():
        value = squares[1]
        for d in range(1, 8):
            arrived(squares_in.at[2 + d], sz + d - 1)
            value = value + squares_in[2 + d]
        squares_all[...] = lax.rsqrt(value / D + 1e-05)

    push(PUSH[2])
    send(wd_hbm.at[others], wd.at[yh], dev(dy=1), w_id + 8)
    for k, (dy, dh, ds) in enumerate(group8):
        arrived(scaled.at[ys[dy], quarter(dh, ds)], q2 + k)

    rows = jnp.concatenate([scaled[0].reshape(384, 256), scaled[1].reshape(384, 256)], axis=1)
    xa1, xa2, xa3 = ids(4), ids(4), ids(4)
    zb = ids(16)
    zra = ids(14)
    xyr = ids(6)
    weight = (wg, wu)
    back = [lax.rem(x + 4 - d, 4) for d in range(4)]
    def multiply(u, c, count):
        columns = weight[u][:, :, 128 * c : 128 * (c + count)].reshape(512, 128 * count)
        value = jnp.dot(rows, columns, preferred_element_type=F32).astype(BF)
        return [value[:, 128 * i : 128 * i + 128] for i in range(count)]

    def multiply_a(u):
        for c in range(0, NA, 2):
            for i, value in enumerate(multiply(u, c, 2)):
                pa[u, :, :, c + i] = value.reshape(4, 2, 48, 128)
        send(pa.at[u, xs[2], 0], pa_in1.at[u, 0], dev(dx=1), xa1 + 2 * u)
        send(pa.at[u, xs[2], 1], pa_in1.at[u, 1], dev(dx=-1), xa1 + 2 * u + 1)
        send(pa.at[u, xs[1], 1], pa_in2.at[u, 0, 1], dev(dx=1), xa2 + 2 * u)
        send(pa.at[u, xs[3], 0], pa_in2.at[u, 1, 0], dev(dx=-1), xa2 + 2 * u + 1)

    def half(towards):
        return pl.ds(0 if towards > 0 else FLAT // 2, FLAT // 2)

    def z_block(u, dist, towards):
        there = lax.rem(z + 8 + towards * dist, 8)
        if dist == 4:
            return pb.at[u, there, half(towards)]
        return pb.at[u, there]

    def z_in(u, dist, towards):
        dst = pb_in.at[u, 0 if towards > 0 else 1, dist - 1]
        if dist == 4:
            return dst.at[half(towards)]
        return dst

    def z_id(u, dist, towards):
        return zb + 8 * u + 2 * (dist - 1) + (0 if towards > 0 else 1)

    def z_send(u, dist):
        for t in (1, -1):
            send(z_block(u, dist, t), z_in(u, dist, t), dev(dz=t), z_id(u, dist, t))

    def multiply_b(u):
        for c in range(0, NB, 2):
            for i, value in enumerate(multiply(u, NA + c, min(2, NB - c))):
                pb[u, :, 48 * (c + i) : 48 * (c + i) + 48] = value.reshape(8, 48, 128)
        pb[u, :, 48 * NB :] = jnp.zeros((8, FLAT - 48 * NB, 128), BF)
        z_send(u, 4)

    def z_step(u, dist):
        for t in (1, -1):
            arrived(z_in(u, dist, t), z_id(u, dist, t))
            there = lax.rem(z + 8 + t * (dist - 1), 8)
            d = 0 if t > 0 else 1
            part_rows = half(t) if dist == 4 else pl.ds(0, FLAT)
            pb[u, there, part_rows] = (
                pb[u, there, part_rows].astype(F32) + pb_in[u, d, dist - 1, part_rows].astype(F32)
            ).astype(BF)
        z_send(u, dist - 1)

    def x_step(u):
        arrived(pa_in1.at[u, 0], xa1 + 2 * u)
        pa[u, xs[1], 0] = (pa[u, xs[1], 0].astype(F32) + pa_in1[u, 0].astype(F32)).astype(BF)
        send(pa.at[u, xs[1], 0], pa_in2.at[u, 0, 0], dev(dx=1), xa3 + 2 * u)
        arrived(pa_in1.at[u, 1], xa1 + 2 * u + 1)
        pa[u, xs[3], 1] = (pa[u, xs[3], 1].astype(F32) + pa_in1[u, 1].astype(F32)).astype(BF)
        send(pa.at[u, xs[3], 1], pa_in2.at[u, 1, 1], dev(dx=-1), xa3 + 2 * u + 1)

    def x_done(u):
        arrived(pa_in2.at[u, 0, 1], xa2 + 2 * u)
        arrived(pa_in2.at[u, 1, 0], xa2 + 2 * u + 1)
        arrived(pa_in2.at[u, 0, 0], xa3 + 2 * u)
        arrived(pa_in2.at[u, 1, 1], xa3 + 2 * u + 1)
        for k in range(2):
            za[u, k] = (
                pa[u, x, k].astype(F32) + pa_in2[u, 0, k].astype(F32) + pa_in2[u, 1, k].astype(F32)
            ).astype(BF)
        for d in range(1, 8):
            send(za.at[u, :, zs[d]], za_in.at[u, d - 1], dev(dz=d), zra + 7 * u + d - 1)

    def own_flat(nx):
        return pl.ds(pl.multiple_of(FLAT // 4 * nx, FLAT // 4), FLAT // 4)

    def xb_start(u):
        for t in (1, -1):
            arrived(z_in(u, 1, t), z_id(u, 1, t))
        xb[u] = (
            pb[u, z].astype(F32) + pb_in[u, 0, 0].astype(F32) + pb_in[u, 1, 0].astype(F32)
        ).astype(BF)
        for j in range(1, 4):
            send(xb.at[u, own_flat(xs[j])], xb_in.at[u, j - 1], dev(dx=j), xyr + 3 * u + j - 1)

    squares_x()
    loads[1].wait()
    loads[2].wait()
    for u in range(2):
        for k in range(4):
            arrived(weight[u].at[1 - yh, pl.ds(64 * k, 64)], w_id + 4 * u + k)
        multiply_a(u)
        multiply_b(u)
    z_step(0, 4)
    x_step(0)
    z_step(1, 4)
    x_step(1)
    z_step(0, 3)
    z_step(1, 3)
    squares_z()
    x_done(0)
    z_step(0, 2)
    z_step(1, 2)
    x_done(1)
    squares_done()
    xb_start(0)
    xb_start(1)

    def scaling(index, offset, count):
        lane_scale = squares_all[pl.ds(index, 1)]
        pick = (
            lax.broadcasted_iota(jnp.int32, (count, 128), 0) + offset
            == lax.broadcasted_iota(jnp.int32, (count, 128), 1)
        )
        return jnp.sum(jnp.where(pick, lane_scale, 0.0), axis=1, keepdims=True)

    def activate(gate, upper, scale):
        gate = gate * scale
        return (gate / (1.0 + jnp.exp(-gate)) * (upper * scale)).astype(BF)

    ga, gax = ids(8), ids(24)
    gb, gbz = ids(4), ids(8)

    scale_rows[...] = jnp.broadcast_to(scaling(z // 2, 48 * lax.rem(z, 2), 48), (48, 128)).reshape(3, 16, 128)
    sums = []
    for u in range(2):
        value = xb[u, own_flat(x)].astype(F32)
        for j in range(3):
            arrived(xb_in.at[u, j], xyr + 3 * u + j)
            value = value + xb_in[u, j].astype(F32)
        sums.append(value)
    tiles = [scale_rows[lax.rem(4 * x + i, 3)] for i in range(4)]
    act_b[z, own_flat(x)] = activate(sums[0], sums[1], jnp.concatenate(tiles, axis=0))
    for j in range(1, 4):
        send(act_b.at[z, own_flat(x)], act_b.at[z, own_flat(x)], dev(dx=j), gb + j)

    sums = []
    for u in range(2):
        value = za[u, :, z].astype(F32)
        for d in range(1, 8):
            arrived(za_in.at[u, d - 1], zra + 7 * u + d - 1)
            value = value + za_in[u, d - 1].astype(F32)
        sums.append(value.reshape(96, 128))
    act_a[x, z] = activate(sums[0], sums[1], scaling(x, 0, 96))
    for d in range(1, 8):
        send(act_a.at[x, z], act_a.at[x, z], dev(dz=d), ga + d)
    for j in range(1, 4):
        send(act_a.at[x, z], act_a.at[x, z], dev(dx=j), gax + j - 1)

    for j in range(1, 4):
        arrived(act_b.at[z, own_flat(back[j])], gb + j)

    def gz(step, towards, shift):
        src = lax.rem(z + 8 - towards * (step - 1 + shift), 8)
        if step == 4:
            return act_b.at[src, half(towards)]
        return act_b.at[src]

    def gz_id(step, towards):
        return gbz + 2 * step + (0 if towards > 0 else 1)

    for t in (1, -1):
        send(gz(1, t, 0), gz(1, t, 0), dev(dz=t), gz_id(0, t))

    def a_step(d):
        nz = zs[(8 - d) % 8]
        arrived(act_a.at[x, nz], ga + d)
        for j in range(1, 4):
            send(act_a.at[x, nz], act_a.at[x, nz], dev(dx=j), gax + 3 * d + j - 1)

    for step in range(1, 5):
        for d in plan[step]:
            a_step(d)
        for t in (1, -1):
            arrived(gz(step, t, 1), gz_id(step - 1, t))
            if step < 4:
                send(gz(step + 1, t, 0), gz(step + 1, t, 0), dev(dz=t), gz_id(step, t))

    loads[3].wait()
    arrived(wd.at[1 - yh], w_id + 8)

    def lower(chunks, first):
        for i in range(0, len(chunks), 2):
            pieces, numbers = zip(*chunks[i : i + 2])
            piece = jnp.concatenate(pieces, axis=1) if len(pieces) == 2 else pieces[0]
            depth = pl.ds(128 * numbers[0], 128 * len(numbers))
            for ny in range(2):
                value = jnp.dot(piece, wd[ny, depth], preferred_element_type=F32).reshape(4, 96, 256)
                if first and i == 0:
                    down[ny] = value
                else:
                    down[ny] += value

    lower([(act_b[:, 48 * c : 48 * c + 48].reshape(384, 128), NA + c) for c in range(NB)], True)
    for d in range(8):
        for j in range(1, 4):
            arrived(act_a.at[back[j], zs[(8 - d) % 8]], gax + 3 * d + j - 1)
    lower([(act_a[:, c].reshape(384, 128), c) for c in range(NA)], False)
    down_bf[...] = down[...].astype(BF)

    q3 = ids(7)
    for k, (dy, dh, ds) in enumerate(group8):
        send(down_bf.at[ys[dy], quarter(dh, ds)], down_in.at[k], dev(dy=dy, dh=dh, ds=ds), q3 + k)
    total = hidden[...] + down[yh, mine]
    for k in range(7):
        arrived(down_in.at[k], q3 + k)
        total = total + down_in[k].astype(F32)
    fin[0] = total[:, :128]
    fin[1] = total[:, 128:]

    for r in range(3):
        for j in range(2):
            send1[pl.ds(2 * r + j, 32, stride=8), :] = fin[j, pl.ds(r, 32, stride=3), :]
    for j in range(2):
        send1[pl.ds(6 + j, 32, stride=8), :] = jnp.zeros((32, 128), F32)
    blocks = send1.reshape(4, 8, 8, 128)
    f1 = ids(7)
    for d in range(1, 8):
        send(blocks.at[:, zs[d]], mid.at[z], dev(dz=d), f1 + d - 1)
    mid[z] = blocks[:, z]
    for d in range(1, 8):
        arrived(mid.at[lax.rem(z + 8 - d, 8)], f1 + d - 1)

    f2 = ids(16)
    for xl in range(2):
        for ny in range(2):
            for nh in range(2):
                nx = 2 * h + xl
                own = (nx == x) & (ny == yh) & (nh == h)

                @pl.when(own)
                def _():
                    out[xy] = mid[:, 2 * xl + ny]

                send(
                    mid.at[:, 2 * xl + ny], out.at[xy], ((nx * 2 + ny) * 8 + z, nh, s),
                    f2 + 4 * xl + 2 * ny + nh, jnp.logical_not(own), slot=f2 + xy,
                )
    for k in range(8):
        own = (xy == k) & (h == x // 2)

        @pl.when(jnp.logical_not(own))
        def _():
            arrived(out.at[k], f2 + k)

    for ref, index, condition in pending:
        when(condition, lambda: copy_of(ref, ref, dev(dh=1), index, index).wait_send())
    assert counter[0] <= SEMS


SEMS = 320


def layer(
    lengths, queries, new_keys, new_values, key_cache, value_cache,
    residual, gain, out_weight, gate_weight, up_weight, down_weight,
):
    vmem = pl.BlockSpec(memory_space=pltpu.VMEM)
    anywhere = pl.BlockSpec(memory_space=pl.ANY)
    scratch = [
        pltpu.VMEM((3, 2048, 256), BF),
        pltpu.VMEM((3, 2048, 256), BF),
        pltpu.VMEM((3, 2, 16, HS), BF),
        pltpu.VMEM((2048, 256), BF),
        pltpu.VMEM((2, 256, UNITS), BF),
        pltpu.VMEM((2, 256, UNITS), BF),
        pltpu.VMEM((2, UNITS, 256), BF),
        pltpu.VMEM((2, 64, 3, 16, HS), BF),
        pltpu.VMEM((64 * 3 * 16, HS), F32),
        pltpu.VMEM((4, 96, 256), F32),
        pltpu.VMEM((4, 96, 256), BF),
        pltpu.VMEM((3, 96, 256), BF),
        pltpu.VMEM((96, 256), F32),
        pltpu.VMEM((2, 4, 96, 256), BF),
        pltpu.VMEM((2, 4, 8, 128), F32),
        pltpu.VMEM((2, 8, 128), F32),
        pltpu.VMEM((10, 8, 128), F32),
        pltpu.VMEM((8, 128), F32),
        pltpu.VMEM((2, 4, 2, NA, 48, 128), BF),
        pltpu.VMEM((2, 2, NA, 48, 128), BF),
        pltpu.VMEM((2, 2, 2, NA, 48, 128), BF),
        pltpu.VMEM((2, 2, NA, 48, 128), BF),
        pltpu.VMEM((2, 7, 2, 48, 128), BF),
        pltpu.VMEM((2, 8, FLAT, 128), BF),
        pltpu.VMEM((2, 2, 4, FLAT, 128), BF),
        pltpu.VMEM((2, FLAT, 128), BF),
        pltpu.VMEM((2, 3, FLAT // 4, 128), BF),
        pltpu.VMEM((3, 16, 128), F32),
        pltpu.VMEM((4, NA, 96, 128), BF),
        pltpu.VMEM((8, FLAT, 128), BF),
        pltpu.VMEM((2, 4, 96, 256), F32),
        pltpu.VMEM((2, 4, 96, 256), BF),
        pltpu.VMEM((7, 96, 256), BF),
        pltpu.VMEM((2, 96, 128), F32),
        pltpu.VMEM((256, 128), F32),
        pltpu.VMEM((8, 4, 8, 128), F32),
        pltpu.SemaphoreType.DMA((6,)),
        pltpu.SemaphoreType.DMA((4,)),
        pltpu.SemaphoreType.DMA((SEMS,)),
        pltpu.SemaphoreType.DMA((SEMS,)),
    ]
    return pl.pallas_call(
        layer_kernel,
        out_shape=jax.ShapeDtypeStruct((8, 8, 8, 128), F32),
        in_specs=[pl.BlockSpec(memory_space=pltpu.SMEM), vmem, vmem, vmem, anywhere, anywhere, vmem, vmem] + [anywhere] * 4,
        out_specs=vmem,
        scratch_shapes=scratch,
        compiler_params=pltpu.CompilerParams(collective_id=0, has_side_effects=True, vmem_limit_bytes=VMEM_LIMIT),
        cost_estimate=pl.CostEstimate(flops=2 * 384 * 256 * 12032, bytes_accessed=8 * 2**20, transcendentals=0),
        name="layer",
    )(lengths, queries, new_keys, new_values, key_cache, value_cache, residual.reshape(4, 96, 256), gain, out_weight, gate_weight, up_weight, down_weight)


def body(
    queries,
    new_keys,
    new_values,
    key_cache,
    value_cache,
    cache_lengths,
    residual,
    norm_gain,
    out_weight,
    gate_weight,
    up_weight,
    down_weight,
):
    rows = layer(
        cache_lengths, queries[0], new_keys[0], new_values[0], key_cache[0], value_cache[0],
        residual, norm_gain, out_weight, gate_weight, up_weight, down_weight,
    )
    rows = rows.reshape(64, 8, HS)[:, :6].reshape(64, 3, 2 * HS)
    return rows.transpose(1, 0, 2).reshape(1, 3, D).astype(BF)


def solution(mesh):
    return jax.shard_map(
        body,
        mesh=mesh,
        in_specs=(
            P("side", "dp", "head"),
            P("side", "dp", "head"),
            P("side", "dp", "head"),
            P("side", "dp", None, "head"),
            P("side", "dp", None, "head"),
            P("side", "dp"),
            P(None, None, "dp"),
            P("dp"),
            P(("head", "side"), "dp"),
            P("dp", ("head", "side")),
            P("dp", ("head", "side")),
            P(("head", "side"), "dp"),
        ),
        out_specs=P("side", "dp", None),
        check_vma=False,
    )
```

time: 152 us -> 133 us (0.88)
  Pallas kernels: 145 us -> 131 us
  local copies, waits for them, and re-layouts: 5.9 us -> 0.75 us
    pallas_call x2 -> x1, Pallas kernels: 145 us -> 131 us  [layer(): pl.pallas_call(layer_kernel, out_shape=jax.ShapeDtypeStruct((8, 8, 8, 128...]
    reshape x3 -> x0, local copies, waits for them, and re-layouts: 3.78 us -> none  [the longest x1 1.28 us: attend(): new_keys.reshape(rows, 1, 2 * HS)]
where the time goes in v2:
time: 133 us
  Pallas kernels  131 us (98%)
    pallas_call x1, Pallas kernels, layer(): pl.pallas_call(layer_kernel, out_shape=jax.ShapeDtypeStruct((8, 8, 8, 128...  131 us

profile of v2, /device:TPU:1, one launch (start us, length us, event | category | flops | bytes accessed | tf_op | source)
XLA Modules:
  0.0 132.9 jit_solution(2320913092109611357)
XLA Ops:
  0.0 131.2 %layer.1 = f32[8,8,8,128]{3,2,1,0:T(8,128)} custom-call(s32[1,3]{1,0:T(1,128)} %lengths.1, bf16[3,4096]{1,0:T(4,128)(2,1)} %bitcast.15, bf16[3,256]{1,0:T(4,128)(2,1)} %bitcast.16, bf16[3,256]{1,0:T(4,128)(2,1)} %bitcast.17, bf16[3,2048,256]{2,1,0:T(8,128)(2,1)} %bitcast.11, bf16[3,2048,256]{2,1,0:T(8,128)(2,1)} %bitcast.12, bf16[4,96,256]{2,1,0:T(8,128)(2,1)} %bitcast.14, ...), custom_call_target="tpu_custom_call" | custom-call | flops 2365587456 | bytes 8388608 | tf_op jit(solution)/shard_map/layer/pallas_call | solution.py:621
  131.2 1.0 convert.4
  132.1 0.8 convert_element_type.18

commit v3 on v2

--- a/solution.py
+++ b/solution.py
@@ -17,7 +17,7 @@
 UNITS = 1664
 NA = 8
 NB = 5
-PUSH = (1, 5, 2)
+PUSH = (1, 4, 1)
 FLAT = 256
 
 
@@ -53,7 +53,7 @@
     squares_mine, squares, squares_in, squares_all,
     pa, pa_in1, pa_in2, za, za_in,
     pb, pb_in, xb, xb_in, scale_rows,
-    act_a, act_b, down, down_bf, down_in, fin, send1, mid,
+    act_a, act_b, down, down_bf, down_in, fin, send1, send1_bf, mid, mid_wide, send2, final, final_wide,
     csem, wsem, ss, rs,
 ):
     dp = lax.axis_index("dp")
@@ -122,10 +122,15 @@
 
     units = pl.ds(pl.multiple_of(UNITS * yh, 128), UNITS)
     others = pl.ds(pl.multiple_of(UNITS * (1 - yh), 128), UNITS)
-    w_id = ids(9)
+    w_id = ids(7)
+    cuts = [(u, 128 * NA, 128 * NB) for u in range(2)]
+    cuts += [(u, 64 * NA * k, 64 * NA) for u in range(2) for k in range(2)]
     pieces = [
-        (src.at[pl.ds(64 * k, 64), others], dst.at[yh, pl.ds(64 * k, 64)])
-        for src, dst in ((wg_hbm, wg), (wu_hbm, wu)) for k in range(4)
+        (
+            (wg_hbm, wu_hbm)[u].at[:, pl.ds(pl.multiple_of(UNITS * (1 - yh) + first, 128), count)],
+            (wg, wu)[u].at[yh, :, pl.ds(first, count)],
+        )
+        for u, first, count in cuts
     ]
     pushed = [0]
 
@@ -140,6 +145,9 @@
         q = jnp.concatenate([q[:, HS * g : HS * g + HS] for g in range(32)], axis=0)
         caches[2 * r].wait()
         caches[2 * r + 1].wait()
+        if r == 0:
+            pl.semaphore_wait(barrier, len(peers))
+            push(PUSH[0])
         if r == 2:
             load(wo_hbm, wo)
             load(wg_hbm.at[:, units], wg.at[yh])
@@ -151,9 +159,6 @@
         )
         att[r, 0] = low
         att[r, 1] = high
-        if r == 0:
-            pl.semaphore_wait(barrier, len(peers))
-            push(PUSH[0])
 
     y_id = ids(4)
     for ny in range(2):
@@ -199,36 +204,33 @@
         arrived(seenx.at[lax.rem(x + 4 - j, 4), :, z], xyb_id + j)
     seenz = seen.at[1].reshape(8, 8, 3, 16, HS)
 
-    def ring(step, towards):
-        src = lax.rem(z + 8 - towards * (step - 1), 8)
-        if step == 4:
-            return seenz.at[pl.ds(0 if towards > 0 else 4, 4), src]
-        return seenz.at[:, src]
-
-    def ring_in(step, towards):
-        src = lax.rem(z + 8 - towards * step, 8)
-        if step == 4:
-            return seenz.at[pl.ds(0 if towards > 0 else 4, 4), src]
-        return seenz.at[:, src]
-
-    def ring_id(step, towards):
-        return zb_id + step * 2 + (0 if towards > 0 else 1)
-
-    for t in (1, -1):
-        send(ring(1, t), ring(1, t), dev(dz=t), ring_id(0, t))
-
-    a_order = [1, 7, 2, 6, 3, 5, 4]
-    plan = {1: a_order[:2], 2: a_order[2:4], 3: a_order[4:6], 4: a_order[6:]}
+    def ring(step, towards, which):
+        return seenz.at[pl.ds(4 * which, 4), lax.rem(z + 8 - towards * (step - 1), 8)]
+
+    def ring_id(step, towards, which):
+        return zb_id + step * 4 + 2 * which + (0 if towards > 0 else 1)
+
+    def last(towards):
+        return 0 if towards > 0 else 1
+
+    for which in range(2):
+        for t in (1, -1):
+            send(ring(1, t, which), ring(1, t, which), dev(dz=t), ring_id(0, t, which))
+
+    plan = {1: (1, 7), 2: (2, 6), 3: (3, 5), 4: (4,)}
     for step in range(1, 5):
         for d in plan[step]:
-            nz = lax.rem(z + 8 - d, 8)
+            nz = zs[8 - d]
             arrived(pair_ref(x, nz), za_id + d)
             for j in range(1, 4):
                 send(pair_ref(x, nz), pair_ref(x, nz), dev(dx=j), xa_id + 3 * d + j - 1)
-        for t in (1, -1):
-            arrived(ring_in(step, t), ring_id(step - 1, t))
-            if step < 4:
-                send(ring(step + 1, t), ring(step + 1, t), dev(dz=t), ring_id(step, t))
+        for which in range(2):
+            for t in (1, -1):
+                if step == 4 and which != last(t):
+                    continue
+                arrived(ring(step + 1, t, which), ring_id(step - 1, t, which))
+                if step < 3 or (step == 3 and which == last(t)):
+                    send(ring(step + 1, t, which), ring(step + 1, t, which), dev(dz=t), ring_id(step, t, which))
 
     loads[0].wait()
 
@@ -304,8 +306,6 @@
             value = value + squares_in[2 + d]
         squares_all[...] = lax.rsqrt(value / D + 1e-05)
 
-    push(PUSH[2])
-    send(wd_hbm.at[others], wd.at[yh], dev(dy=1), w_id + 8)
     for k, (dy, dh, ds) in enumerate(group8):
         arrived(scaled.at[ys[dy], quarter(dh, ds)], q2 + k)
 
@@ -403,20 +403,29 @@
             send(xb.at[u, own_flat(xs[j])], xb_in.at[u, j - 1], dev(dx=j), xyr + 3 * u + j - 1)
 
     squares_x()
+    push(PUSH[2])
     loads[1].wait()
     loads[2].wait()
+    def weights_there(*numbers):
+        for k in numbers:
+            u, first, count = cuts[k]
+            arrived(weight[u].at[1 - yh, :, pl.ds(first, count)], w_id + k)
+
     for u in range(2):
-        for k in range(4):
-            arrived(weight[u].at[1 - yh, pl.ds(64 * k, 64)], w_id + 4 * u + k)
-        multiply_a(u)
+        weights_there(u)
         multiply_b(u)
+    weights_there(2, 3)
+    multiply_a(0)
     z_step(0, 4)
+    z_step(1, 4)
+    weights_there(4, 5)
+    send(wd_hbm.at[others], wd.at[yh], dev(dy=1), w_id + 6)
+    multiply_a(1)
     x_step(0)
-    z_step(1, 4)
-    x_step(1)
     z_step(0, 3)
     z_step(1, 3)
     squares_z()
+    x_step(1)
     x_done(0)
     z_step(0, 2)
     z_step(1, 2)
@@ -469,17 +478,12 @@
     for j in range(1, 4):
         arrived(act_b.at[z, own_flat(back[j])], gb + j)
 
-    def gz(step, towards, shift):
-        src = lax.rem(z + 8 - towards * (step - 1 + shift), 8)
-        if step == 4:
-            return act_b.at[src, half(towards)]
-        return act_b.at[src]
-
-    def gz_id(step, towards):
-        return gbz + 2 * step + (0 if towards > 0 else 1)
+    def gz_id(dist, towards):
+        return gbz + 2 * (dist - 1) + (0 if towards > 0 else 1)
 
     for t in (1, -1):
-        send(gz(1, t, 0), gz(1, t, 0), dev(dz=t), gz_id(0, t))
+        for dist in (2, 1):
+            send(act_b.at[z], act_b.at[z], dev(dz=t * dist), gz_id(dist, t))
 
     def a_step(d):
         nz = zs[(8 - d) % 8]
@@ -487,16 +491,22 @@
         for j in range(1, 4):
             send(act_a.at[x, nz], act_a.at[x, nz], dev(dx=j), gax + 3 * d + j - 1)
 
-    for step in range(1, 5):
-        for d in plan[step]:
-            a_step(d)
-        for t in (1, -1):
-            arrived(gz(step, t, 1), gz_id(step - 1, t))
-            if step < 4:
-                send(gz(step + 1, t, 0), gz(step + 1, t, 0), dev(dz=t), gz_id(step, t))
+    a_step(1)
+    a_step(7)
+    for t in (1, -1):
+        far = act_b.at[zs[(8 - 2 * t) % 8]]
+        arrived(far, gz_id(2, t))
+        send(far, far, dev(dz=t), gz_id(3, t))
+        send(far.at[half(t)], far.at[half(t)], dev(dz=2 * t), gz_id(4, t))
+    for d in (2, 6, 3, 5, 4):
+        a_step(d)
+    for t in (1, -1):
+        arrived(act_b.at[zs[(8 - t) % 8]], gz_id(1, t))
+        arrived(act_b.at[zs[(8 - 3 * t) % 8]], gz_id(3, t))
+        arrived(act_b.at[zs[4], half(t)], gz_id(4, t))
 
     loads[3].wait()
-    arrived(wd.at[1 - yh], w_id + 8)
+    arrived(wd.at[1 - yh], w_id + 6)
 
     def lower(chunks, first):
         for i in range(0, len(chunks), 2):
@@ -529,16 +539,22 @@
 
     for r in range(3):
         for j in range(2):
-            send1[pl.ds(2 * r + j, 32, stride=8), :] = fin[j, pl.ds(r, 32, stride=3), :]
-    for j in range(2):
-        send1[pl.ds(6 + j, 32, stride=8), :] = jnp.zeros((32, 128), F32)
-    blocks = send1.reshape(4, 8, 8, 128)
+            value = fin[j, pl.ds(r, 32, stride=3), :]
+            for k in range(4):
+                send1[pl.ds((2 * r + j) * 4 + k, 8, stride=32), :] = value[8 * k : 8 * k + 8]
+    for k in range(8):
+        send1[pl.ds(24 + k, 8, stride=32), :] = jnp.zeros((8, 128), F32)
+    send1_bf[...] = send1[...].astype(BF).reshape(8, 32, 128)
     f1 = ids(7)
     for d in range(1, 8):
-        send(blocks.at[:, zs[d]], mid.at[z], dev(dz=d), f1 + d - 1)
-    mid[z] = blocks[:, z]
+        send(send1_bf.at[zs[d]], mid.at[z], dev(dz=d), f1 + d - 1)
+    mid[z] = send1_bf[z]
     for d in range(1, 8):
-        arrived(mid.at[lax.rem(z + 8 - d, 8)], f1 + d - 1)
+        arrived(mid.at[zs[8 - d]], f1 + d - 1)
+    mid_wide[...] = mid[...].astype(F32).reshape(256, 128)
+    for k in range(4):
+        rows_k = [mid_wide[pl.ds(4 * i + k, 8, stride=32), :] for i in range(6)]
+        send2[k] = jnp.concatenate(rows_k, axis=0).astype(BF)
 
     f2 = ids(16)
     for xl in range(2):
@@ -549,10 +565,10 @@
 
                 @pl.when(own)
                 def _():
-                    out[xy] = mid[:, 2 * xl + ny]
+                    final[xy] = send2[2 * xl + ny]
 
                 send(
-                    mid.at[:, 2 * xl + ny], out.at[xy], ((nx * 2 + ny) * 8 + z, nh, s),
+                    send2.at[2 * xl + ny], final.at[xy], ((nx * 2 + ny) * 8 + z, nh, s),
                     f2 + 4 * xl + 2 * ny + nh, jnp.logical_not(own), slot=f2 + xy,
                 )
     for k in range(8):
@@ -560,7 +576,12 @@
 
         @pl.when(jnp.logical_not(own))
         def _():
-            arrived(out.at[k], f2 + k)
+            arrived(final.at[k], f2 + k)
+
+    final_wide[...] = final[...].astype(F32).reshape(384, 128)
+    for k in range(8):
+        columns = [final_wide[pl.ds(48 * k + 8 * j + i, 3, stride=16), :] for i in range(8) for j in range(2)]
+        out[:, 2048 * k : 2048 * k + 2048] = jnp.concatenate(columns, axis=1).astype(BF)
 
     for ref, index, condition in pending:
         when(condition, lambda: copy_of(ref, ref, dev(dh=1), index, index).wait_send())
@@ -612,7 +633,12 @@
         pltpu.VMEM((7, 96, 256), BF),
         pltpu.VMEM((2, 96, 128), F32),
         pltpu.VMEM((256, 128), F32),
-        pltpu.VMEM((8, 4, 8, 128), F32),
+        pltpu.VMEM((8, 32, 128), BF),
+        pltpu.VMEM((8, 32, 128), BF),
+        pltpu.VMEM((256, 128), F32),
+        pltpu.VMEM((4, 48, 128), BF),
+        pltpu.VMEM((8, 48, 128), BF),
+        pltpu.VMEM((384, 128), F32),
         pltpu.SemaphoreType.DMA((6,)),
         pltpu.SemaphoreType.DMA((4,)),
         pltpu.SemaphoreType.DMA((SEMS,)),
@@ -620,7 +646,7 @@
     ]
     return pl.pallas_call(
         layer_kernel,
-        out_shape=jax.ShapeDtypeStruct((8, 8, 8, 128), F32),
+        out_shape=jax.ShapeDtypeStruct((3, D), BF),
         in_specs=[pl.BlockSpec(memory_space=pltpu.SMEM), vmem, vmem, vmem, anywhere, anywhere, vmem, vmem] + [anywhere] * 4,
         out_specs=vmem,
         scratch_shapes=scratch,
@@ -648,8 +674,7 @@
         cache_lengths, queries[0], new_keys[0], new_values[0], key_cache[0], value_cache[0],
         residual, norm_gain, out_weight, gate_weight, up_weight, down_weight,
     )
-    rows = rows.reshape(64, 8, HS)[:, :6].reshape(64, 3, 2 * HS)
-    return rows.transpose(1, 0, 2).reshape(1, 3, D).astype(BF)
+    return rows.reshape(1, 3, D)
 
 
 def solution(mesh):

time: 133 us -> 127 us (0.955)
  Pallas kernels: 131 us -> 125 us
    pallas_call x1, Pallas kernels: 131 us -> 125 us  [layer(): pl.pallas_call(layer_kernel, out_shape=jax.ShapeDtypeStruct((3, D), BF),...]
    unnamed x0 -> x1, local copies, waits for them, and re-layouts: none -> 1.61 us
where the time goes in v3:
time: 127 us
  Pallas kernels  125 us (98%)
  local copies, waits for them, and re-layouts  1.61 us (1%)
    pallas_call x1, Pallas kernels, layer(): pl.pallas_call(layer_kernel, out_shape=jax.ShapeDtypeStruct((3, D), BF),...  125 us

profile of v3, /device:TPU:1, one launch (start us, length us, event | category | flops | bytes accessed | tf_op | source)
XLA Modules:
  0.0 126.7 jit_solution(3372791204778545573)
XLA Ops:
  0.0 125.1 %layer.1 = bf16[3,16384]{1,0:T(4,128)(2,1)} custom-call(s32[1,3]{1,0:T(1,128)} %lengths.1, bf16[3,4096]{1,0:T(4,128)(2,1)} %bitcast.11, bf16[3,256]{1,0:T(4,128)(2,1)} %bitcast.12, bf16[3,256]{1,0:T(4,128)(2,1)} %bitcast.13, bf16[3,2048,256]{2,1,0:T(8,128)(2,1)} %bitcast.7, bf16[3,2048,256]{2,1,0:T(8,128)(2,1)} %bitcast.8, bf16[4,96,256]{2,1,0:T(8,128)(2,1)} %bitcast.10, ...), custom_call_target="tpu_custom_call" | custom-call | flops 2365587456 | bytes 8388608 | tf_op jit(solution)/shard_map/layer/pallas_call | solution.py:647
  125.1 1.6 %copy.14 = bf16[1,3,16384]{2,1,0:T(4,128)(2,1)} copy(bf16[1,3,16384]{2,1,0:T(4,128)(2,1)} %bitcast.9) | data formatting | bytes 196608

commit v4 on v3

--- a/solution.py
+++ b/solution.py
@@ -310,9 +310,9 @@
         arrived(scaled.at[ys[dy], quarter(dh, ds)], q2 + k)
 
     rows = jnp.concatenate([scaled[0].reshape(384, 256), scaled[1].reshape(384, 256)], axis=1)
-    xa1, xa2, xa3 = ids(4), ids(4), ids(4)
+    xa1, xa2, xa3 = ids(8), ids(8), ids(8)
     zb = ids(16)
-    zra = ids(14)
+    zra = ids(16)
     xyr = ids(6)
     weight = (wg, wu)
     back = [lax.rem(x + 4 - d, 4) for d in range(4)]
@@ -321,14 +321,18 @@
         value = jnp.dot(rows, columns, preferred_element_type=F32).astype(BF)
         return [value[:, 128 * i : 128 * i + 128] for i in range(count)]
 
-    def multiply_a(u):
-        for c in range(0, NA, 2):
+    def group_of(g):
+        return g // 2, pl.ds(4 * (g % 2), 4)
+
+    def multiply_a(g):
+        u, some = group_of(g)
+        for c in range(4 * (g % 2), 4 * (g % 2) + 4, 2):
             for i, value in enumerate(multiply(u, c, 2)):
                 pa[u, :, :, c + i] = value.reshape(4, 2, 48, 128)
-        send(pa.at[u, xs[2], 0], pa_in1.at[u, 0], dev(dx=1), xa1 + 2 * u)
-        send(pa.at[u, xs[2], 1], pa_in1.at[u, 1], dev(dx=-1), xa1 + 2 * u + 1)
-        send(pa.at[u, xs[1], 1], pa_in2.at[u, 0, 1], dev(dx=1), xa2 + 2 * u)
-        send(pa.at[u, xs[3], 0], pa_in2.at[u, 1, 0], dev(dx=-1), xa2 + 2 * u + 1)
+        send(pa.at[u, xs[2], 0, some], pa_in1.at[u, 0, some], dev(dx=1), xa1 + 2 * g)
+        send(pa.at[u, xs[2], 1, some], pa_in1.at[u, 1, some], dev(dx=-1), xa1 + 2 * g + 1)
+        send(pa.at[u, xs[1], 1, some], pa_in2.at[u, 0, 1, some], dev(dx=1), xa2 + 2 * g)
+        send(pa.at[u, xs[3], 0, some], pa_in2.at[u, 1, 0, some], dev(dx=-1), xa2 + 2 * g + 1)
 
     def half(towards):
         return pl.ds(0 if towards > 0 else FLAT // 2, FLAT // 2)
@@ -370,25 +374,29 @@
             ).astype(BF)
         z_send(u, dist - 1)
 
-    def x_step(u):
-        arrived(pa_in1.at[u, 0], xa1 + 2 * u)
-        pa[u, xs[1], 0] = (pa[u, xs[1], 0].astype(F32) + pa_in1[u, 0].astype(F32)).astype(BF)
-        send(pa.at[u, xs[1], 0], pa_in2.at[u, 0, 0], dev(dx=1), xa3 + 2 * u)
-        arrived(pa_in1.at[u, 1], xa1 + 2 * u + 1)
-        pa[u, xs[3], 1] = (pa[u, xs[3], 1].astype(F32) + pa_in1[u, 1].astype(F32)).astype(BF)
-        send(pa.at[u, xs[3], 1], pa_in2.at[u, 1, 1], dev(dx=-1), xa3 + 2 * u + 1)
-
-    def x_done(u):
-        arrived(pa_in2.at[u, 0, 1], xa2 + 2 * u)
-        arrived(pa_in2.at[u, 1, 0], xa2 + 2 * u + 1)
-        arrived(pa_in2.at[u, 0, 0], xa3 + 2 * u)
-        arrived(pa_in2.at[u, 1, 1], xa3 + 2 * u + 1)
+    def x_step(g):
+        u, some = group_of(g)
+        for k, there in enumerate((xs[1], xs[3])):
+            arrived(pa_in1.at[u, k, some], xa1 + 2 * g + k)
+            pa[u, there, k, some] = (pa[u, there, k, some].astype(F32) + pa_in1[u, k, some].astype(F32)).astype(BF)
+            send(pa.at[u, there, k, some], pa_in2.at[u, k, k, some], dev(dx=1 - 2 * k), xa3 + 2 * g + k)
+
+    def x_done(g):
+        u, some = group_of(g)
+        arrived(pa_in2.at[u, 0, 1, some], xa2 + 2 * g)
+        arrived(pa_in2.at[u, 1, 0, some], xa2 + 2 * g + 1)
+        arrived(pa_in2.at[u, 0, 0, some], xa3 + 2 * g)
+        arrived(pa_in2.at[u, 1, 1, some], xa3 + 2 * g + 1)
         for k in range(2):
-            za[u, k] = (
-                pa[u, x, k].astype(F32) + pa_in2[u, 0, k].astype(F32) + pa_in2[u, 1, k].astype(F32)
+            za[u, k, some] = (
+                pa[u, x, k, some].astype(F32) + pa_in2[u, 0, k, some].astype(F32) + pa_in2[u, 1, k, some].astype(F32)
             ).astype(BF)
-        for d in range(1, 8):
-            send(za.at[u, :, zs[d]], za_in.at[u, d - 1], dev(dz=d), zra + 7 * u + d - 1)
+        for c in range(4 * (g % 2), 4 * (g % 2) + 4):
+            places = lax.rem(c - z + 8, 8)
+            send(
+                za.at[u, :, c], za_in.at[u, places], (xy * 8 + c, h, s), zra + 8 * u + c, z != c,
+                slot=zra + 8 * u + places,
+            )
 
     def own_flat(nx):
         return pl.ds(pl.multiple_of(FLAT // 4 * nx, FLAT // 4), FLAT // 4)
@@ -414,23 +422,30 @@
     for u in range(2):
         weights_there(u)
         multiply_b(u)
-    weights_there(2, 3)
-    multiply_a(0)
+    for g in range(2):
+        weights_there(2 + g)
+        multiply_a(g)
     z_step(0, 4)
     z_step(1, 4)
-    weights_there(4, 5)
-    send(wd_hbm.at[others], wd.at[yh], dev(dy=1), w_id + 6)
-    multiply_a(1)
+    weights_there(4)
+    multiply_a(2)
     x_step(0)
+    x_step(1)
     z_step(0, 3)
     z_step(1, 3)
+    weights_there(5)
+    multiply_a(3)
+    send(wd_hbm.at[others], wd.at[yh], dev(dy=1), w_id + 6)
     squares_z()
-    x_step(1)
+    x_step(2)
     x_done(0)
+    x_done(1)
     z_step(0, 2)
+    x_step(3)
     z_step(1, 2)
-    x_done(1)
+    x_done(2)
     squares_done()
+    x_done(3)
     xb_start(0)
     xb_start(1)
 
@@ -466,8 +481,8 @@
     for u in range(2):
         value = za[u, :, z].astype(F32)
         for d in range(1, 8):
-            arrived(za_in.at[u, d - 1], zra + 7 * u + d - 1)
-            value = value + za_in[u, d - 1].astype(F32)
+            arrived(za_in.at[u, d], zra + 8 * u + d)
+            value = value + za_in[u, d].astype(F32)
         sums.append(value.reshape(96, 128))
     act_a[x, z] = activate(sums[0], sums[1], scaling(x, 0, 96))
     for d in range(1, 8):
@@ -620,7 +635,7 @@
         pltpu.VMEM((2, 2, NA, 48, 128), BF),
         pltpu.VMEM((2, 2, 2, NA, 48, 128), BF),
         pltpu.VMEM((2, 2, NA, 48, 128), BF),
-        pltpu.VMEM((2, 7, 2, 48, 128), BF),
+        pltpu.VMEM((2, 8, 2, 48, 128), BF),
         pltpu.VMEM((2, 8, FLAT, 128), BF),
         pltpu.VMEM((2, 2, 4, FLAT, 128), BF),
         pltpu.VMEM((2, FLAT, 128), BF),

time: 127 us -> 124 us (0.976)
  Pallas kernels: 125 us -> 122 us
    pallas_call x1, Pallas kernels: 125 us -> 122 us  [layer(): pl.pallas_call(layer_kernel, out_shape=jax.ShapeDtypeStruct((3, D), BF),...]
where the time goes in v4:
time: 124 us
  Pallas kernels  122 us (98%)
  local copies, waits for them, and re-layouts  1.61 us (1%)
    pallas_call x1, Pallas kernels, layer(): pl.pallas_call(layer_kernel, out_shape=jax.ShapeDtypeStruct((3, D), BF),...  122 us

profile of v4, /device:TPU:1, one launch (start us, length us, event | category | flops | bytes accessed | tf_op | source)
XLA Modules:
  0.0 124.0 jit_solution(11939603031518950419)
XLA Ops:
  0.0 122.4 %layer.1 = bf16[3,16384]{1,0:T(4,128)(2,1)} custom-call(s32[1,3]{1,0:T(1,128)} %lengths.1, bf16[3,4096]{1,0:T(4,128)(2,1)} %bitcast.11, bf16[3,256]{1,0:T(4,128)(2,1)} %bitcast.12, bf16[3,256]{1,0:T(4,128)(2,1)} %bitcast.13, bf16[3,2048,256]{2,1,0:T(8,128)(2,1)} %bitcast.7, bf16[3,2048,256]{2,1,0:T(8,128)(2,1)} %bitcast.8, bf16[4,96,256]{2,1,0:T(8,128)(2,1)} %bitcast.10, ...), custom_call_target="tpu_custom_call" | custom-call | flops 2365587456 | bytes 8388608 | tf_op jit(solution)/shard_map/layer/pallas_call | solution.py:662
  122.4 1.6 %copy.14 = bf16[1,3,16384]{2,1,0:T(4,128)(2,1)} copy(bf16[1,3,16384]{2,1,0:T(4,128)(2,1)} %bitcast.9) | data formatting | bytes 196608

commit v5 on v4

--- a/solution.py
+++ b/solution.py
@@ -17,7 +17,7 @@
 UNITS = 1664
 NA = 8
 NB = 5
-PUSH = (1, 4, 1)
+PUSH = (1, 4, 2)
 FLAT = 256
 
 
@@ -122,8 +122,8 @@
 
     units = pl.ds(pl.multiple_of(UNITS * yh, 128), UNITS)
     others = pl.ds(pl.multiple_of(UNITS * (1 - yh), 128), UNITS)
-    w_id = ids(7)
-    cuts = [(u, 128 * NA, 128 * NB) for u in range(2)]
+    w_id = ids(8)
+    cuts = [(0, 128 * NA, 256), (0, 128 * NA + 256, 128 * NB - 256), (1, 128 * NA, 128 * NB)]
     cuts += [(u, 64 * NA * k, 64 * NA) for u in range(2) for k in range(2)]
     pieces = [
         (
@@ -420,22 +420,22 @@
             arrived(weight[u].at[1 - yh, :, pl.ds(first, count)], w_id + k)
 
     for u in range(2):
-        weights_there(u)
+        weights_there(*((0, 1), (2,))[u])
         multiply_b(u)
     for g in range(2):
-        weights_there(2 + g)
+        weights_there(3 + g)
         multiply_a(g)
     z_step(0, 4)
     z_step(1, 4)
-    weights_there(4)
+    weights_there(5)
     multiply_a(2)
     x_step(0)
     x_step(1)
     z_step(0, 3)
     z_step(1, 3)
-    weights_there(5)
+    weights_there(6)
     multiply_a(3)
-    send(wd_hbm.at[others], wd.at[yh], dev(dy=1), w_id + 6)
+    send(wd_hbm.at[others], wd.at[yh], dev(dy=1), w_id + 7)
     squares_z()
     x_step(2)
     x_done(0)
@@ -521,7 +521,7 @@
         arrived(act_b.at[zs[4], half(t)], gz_id(4, t))
 
     loads[3].wait()
-    arrived(wd.at[1 - yh], w_id + 6)
+    arrived(wd.at[1 - yh], w_id + 7)
 
     def lower(chunks, first):
         for i in range(0, len(chunks), 2):

time: 124 us -> 121 us (0.976)
  Pallas kernels: 122 us -> 119 us
    pallas_call x1, Pallas kernels: 122 us -> 119 us  [layer(): pl.pallas_call(layer_kernel, out_shape=jax.ShapeDtypeStruct((3, D), BF),...]
where the time goes in v5:
time: 121 us
  Pallas kernels  119 us (98%)
  local copies, waits for them, and re-layouts  1.61 us (1%)
    pallas_call x1, Pallas kernels, layer(): pl.pallas_call(layer_kernel, out_shape=jax.ShapeDtypeStruct((3, D), BF),...  119 us

profile of v5, /device:TPU:1, one launch (start us, length us, event | category | flops | bytes accessed | tf_op | source)
XLA Modules:
  0.0 121.0 jit_solution(13387918657211009351)
XLA Ops:
  0.0 119.4 %layer.1 = bf16[3,16384]{1,0:T(4,128)(2,1)} custom-call(s32[1,3]{1,0:T(1,128)} %lengths.1, bf16[3,4096]{1,0:T(4,128)(2,1)} %bitcast.11, bf16[3,256]{1,0:T(4,128)(2,1)} %bitcast.12, bf16[3,256]{1,0:T(4,128)(2,1)} %bitcast.13, bf16[3,2048,256]{2,1,0:T(8,128)(2,1)} %bitcast.7, bf16[3,2048,256]{2,1,0:T(8,128)(2,1)} %bitcast.8, bf16[4,96,256]{2,1,0:T(8,128)(2,1)} %bitcast.10, ...), custom_call_target="tpu_custom_call" | custom-call | flops 2365587456 | bytes 8388608 | tf_op jit(solution)/shard_map/layer/pallas_call | solution.py:662
  119.4 1.6 %copy.14 = bf16[1,3,16384]{2,1,0:T(4,128)(2,1)} copy(bf16[1,3,16384]{2,1,0:T(4,128)(2,1)} %bitcast.9) | data formatting | bytes 196608
